TPU v7x, 128 devices: a whole 4x4x4 slice. The times are simulated.
128 devices in a mesh: gx: 8 (over y, z_lo), gy: 16 (over z_hi, x, core).
Axes of the slice: x: 4, y: 4, z: 4 (z_hi: 2, z_lo: 2; z = z_hi * 2 + z_lo), core: 2. Of those that a mesh axis runs over, the one named last changes fastest.
Arguments:
- velocity: float32 [3, 96, 448, 1024], P(None, 'gx', 'gy'), may hold values from -12 to 12
- viscosity: float32 [96, 448, 1024], P('gx', 'gy'), may hold values from 0.5 to 4
- cells: int32 [3, 131072], P(None, ('gx', 'gy')), may hold values from 0 to 1023, as said below
- offsets: float32 [3, 131072], P(None, ('gx', 'gy')), may hold values from 0 to 1
- forces: float32 [3, 131072], P(None, ('gx', 'gy')), may hold values from -48 to 48
- owners: int32 [131072, 1], P(('gx', 'gy')), may hold values from 0 to 127; in each aligned block of 1024 rows (0 to 1023, 1024 to 2047, ...) at most 16 rows name the same one
Outputs:
- new_velocity: float32 [3, 96, 448, 1024], P(None, 'gx', 'gy')
- marker_velocity: float32 [3, 131072], P(None, ('gx', 'gy'))
Inputs may be any that keep to these rules, and one draw needn't show every extreme that they name: cells[0] lies below 12, cells[1] below 28, cells[2] below 1024. `owners`: among one device's 1024 markers at most 16 have the same owner, and in every draw some owner is named exactly 16 times by one device's markers.
All inputs are finite; a program needn't handle non-finite values.
Results may differ from a plain program's by a relative error of at most 0.000096.
Values sent between devices are 32-bit elements; how exact they have to be, the bound alone decides.
No kernel may reach another device: no remote copies, remote signals or barrier semaphores. Data moves between devices by JAX's collectives and lax.ppermute only.
A program may use at most 128 MiB of HBM per device.

v0:
```python
import functools

import jax
import jax.numpy as jnp
from jax import lax
from jax.experimental import pallas as pl
from jax.experimental.pallas import tpu as pltpu
from jax.sharding import PartitionSpec as P

F32 = jnp.float32
BF16 = jnp.bfloat16
I32 = jnp.int32
LIMIT = 60 * 1024 * 1024
CAP = 16
HALO = 3
PAD = 8
YE = 40
VISITS = 16
STEP = 256


def split3(x):
    hi = x.astype(BF16).astype(F32)
    rest = x - hi
    mid = rest.astype(BF16).astype(F32)
    return hi, mid, rest - mid


def split2(x):
    hi = x.astype(BF16)
    return hi, (x - hi.astype(F32)).astype(BF16)


def nn(a, b):
    return lax.dot_general(a, b, (((1,), (0,)), ((), ())), preferred_element_type=F32)


def nt(a, b):
    return lax.dot_general(a, b, (((1,), (1,)), ((), ())), preferred_element_type=F32)


def tn(a, b):
    return lax.dot_general(a, b, (((0,), (0,)), ((), ())), preferred_element_type=F32)


def iota(shape, dim):
    return lax.broadcasted_iota(I32, shape, dim)


def vmem():
    return pl.BlockSpec(memory_space=pltpu.VMEM)


def smem():
    return pl.BlockSpec(memory_space=pltpu.SMEM)


def params():
    return pltpu.CompilerParams(vmem_limit_bytes=LIMIT)


def cost(flops, size):
    return pl.CostEstimate(flops=flops, bytes_accessed=size, transcendentals=0)


def pack_kernel(owner_ref, cells_ref, offsets_ref, forces_ref, out_ref, rank_ref):
    markers = owner_ref.shape[1]
    devices = out_ref.shape[0]
    owner = owner_ref[...]
    before = (iota((128, 128), 0) < iota((128, 128), 1)).astype(BF16)
    running = jnp.zeros((devices, 1), F32)
    ranks = []
    hots = []
    for g in range(markers // 128):
        hot = (iota((devices, 128), 0) == owner[:, g * 128 : (g + 1) * 128]).astype(F32)
        within = nn(hot.astype(BF16), before)
        ranks.append(jnp.sum(hot * (within + running), axis=0, keepdims=True))
        running = running + jnp.sum(hot, axis=1, keepdims=True)
        hots.append(hot.astype(BF16))
    rank = jnp.concatenate(ranks, axis=1).astype(I32)
    rank_ref[...] = rank
    onehot = jnp.concatenate(hots, axis=1)
    payload = jnp.concatenate(
        [
            cells_ref[...].astype(F32),
            offsets_ref[...],
            forces_ref[...],
            jnp.ones((1, markers), F32),
            jnp.zeros((6, markers), F32),
        ],
        axis=0,
    )
    parts = split3(payload)
    total = None
    for part in parts:
        rows = jnp.concatenate([jnp.where(rank == k, part, 0.0) for k in range(CAP)], axis=0)
        term = nt(onehot, rows.astype(BF16))
        total = term if total is None else total + term
    out_ref[...] = total


def pack(owner_row, cells, offsets, forces, devices):
    markers = owner_row.shape[1]
    return pl.pallas_call(
        pack_kernel,
        out_shape=(
            jax.ShapeDtypeStruct((devices, CAP * 16), F32),
            jax.ShapeDtypeStruct((1, markers), I32),
        ),
        in_specs=[vmem()] * 4,
        out_specs=(vmem(), vmem()),
        compiler_params=params(),
        cost_estimate=cost(4 * 10**8, 300_000),
        name="pack",
    )(owner_row, cells, offsets, forces)


def place_block(flat, start, count):
    return (flat == start + iota((count, flat.shape[1]), 0)).astype(F32).astype(BF16)


def sort_kernel(depth, rec_ref, list_ref, rank_ref, keys, pieces):
    devices = rec_ref.shape[0]
    slots = devices * CAP
    rec = rec_ref[...]
    flipped = rec.T
    empty = float(depth * 4096)

    def key_of(z, valid, index):
        low = jnp.where(z < 0.5, float(depth - 1), z - 1.0)
        return jnp.where(valid > 0.5, low * float(slots), empty) + index

    rows = []
    lane = iota((devices, 128), 1)
    for k in range(CAP):
        at = k * 16
        column = key_of(
            rec[:, at + 2 : at + 3],
            rec[:, at + 9 : at + 10],
            (iota((devices, 1), 0) + k * devices).astype(F32),
        )
        keys[k] = jnp.broadcast_to(column, (devices, devices))
        rows.append(
            key_of(
                flipped[at + 2 : at + 3, :],
                flipped[at + 9 : at + 10, :],
                (iota((1, devices), 1) + k * devices).astype(F32),
            )
        )
        half = rec[:, (k // 8) * 128 : (k // 8 + 1) * 128]
        turned = half if k % 8 == 0 else pltpu.roll(half, 128 - (k % 8) * 16, 1)
        hi, mid, lo = split3(turned)
        joined = jnp.where(
            lane < 16,
            hi,
            jnp.where(
                lane < 32, pltpu.roll(mid, 16, 1), jnp.where(lane < 48, pltpu.roll(lo, 32, 1), 0.0)
            ),
        )
        pieces[k * devices : (k + 1) * devices, :] = joined.astype(BF16)
    ranks = []
    for k in range(CAP):
        row = rows[k]

        def count(other, acc):
            return acc + jnp.where(keys[other] < row, 1.0, 0.0)

        acc = lax.fori_loop(0, CAP, count, jnp.zeros((devices, devices), F32))
        ranks.append(jnp.sum(acc, axis=0, keepdims=True).astype(I32))
    rank_ref[...] = jnp.concatenate(ranks, axis=0)
    flat = jnp.concatenate(ranks, axis=1)
    block = 256
    for b in range(slots // block):
        moved = nn(place_block(flat, b * block, block), pieces[...]).T
        rows = moved[0:16] + moved[16:32] + moved[32:48]
        z = rows[2:3]
        low = jnp.where(z < 0.5, float(depth - 1), z - 1.0)
        list_ref[:, b * block : (b + 1) * block] = jnp.where(
            iota((16, block), 0) == 2, low, rows
        )
    low = jnp.where(list_ref[9:10, :] > 0.5, list_ref[2:3, :], float(4 * depth))
    visit = (iota((VISITS, slots), 0) * 128).astype(F32)
    diagonal = iota((VISITS, 128), 0) == iota((VISITS, 128), 1)

    def count_below(bound):
        column = jnp.sum(jnp.where(low < bound, 1.0, 0.0), axis=1, keepdims=True)
        return jnp.sum(jnp.where(diagonal, column, 0.0), axis=0, keepdims=True)

    first = count_below(visit - 3.0)
    last = count_below(visit + 128.0)
    meta = jnp.where(iota((1, 128), 1) < VISITS, first, pltpu.roll(last, VISITS, 1))
    list_ref[10:11, 0:128] = meta


def sort(received, depth):
    devices = received.shape[0]
    slots = devices * CAP
    return pl.pallas_call(
        functools.partial(sort_kernel, depth),
        out_shape=(
            jax.ShapeDtypeStruct((16, slots), F32),
            jax.ShapeDtypeStruct((CAP, devices), I32),
        ),
        in_specs=[vmem()],
        out_specs=(vmem(), vmem()),
        scratch_shapes=[
            pltpu.VMEM((CAP, devices, devices), F32),
            pltpu.VMEM((slots, 128), BF16),
        ],
        compiler_params=params(),
        cost_estimate=cost(2 * 10**9, 300_000),
        name="sort",
    )(received)


def bump(frac):
    root = jnp.sqrt(1.0 + 4.0 * frac - 4.0 * frac * frac)
    return (
        (3.0 - 2.0 * frac - root) / 8.0,
        (3.0 - 2.0 * frac + root) / 8.0,
        (1.0 + 2.0 * frac + root) / 8.0,
        (1.0 + 2.0 * frac - root) / 8.0,
    )


def tent(first, weights, count, modulus=None):
    rows = iota((count, first.shape[1]), 0)
    table = 0.0
    for i in range(4):
        target = first + i
        if modulus is not None:
            target = jnp.bitwise_and(target, modulus - 1)
        table = jnp.where(rows == target, weights[i], table)
    return table


def markers_of(meta, index, visit, step, ref, at):
    slots = ref.shape[2]
    width = STEP + 128
    start = meta[index, visit] + STEP * step
    chunk = jnp.minimum(lax.shift_right_logical(start, 7), slots // 128 - width // 128)
    ahead = start - chunk * 128
    lanes = pl.ds(pl.multiple_of(chunk * 128, 128), width)
    part = pltpu.roll(ref[at, :, lanes], jnp.where(ahead == 0, 0, width - ahead), 1)[:, 0:STEP]
    live = iota((1, STEP), 1) < meta[index, VISITS + visit] - start
    return part, lanes, ahead, live


def window_of(part, live, window, depth):
    weights = [jnp.where(live, w, 0.0) for w in bump(part[5:6])]
    return tent(part[2:3].astype(I32) - window * 128, weights, 128, depth)


def plane_of(part, shift_x, rows_x, shift_y, rows_y):
    table_x = tent(part[0:1].astype(I32) + shift_x, bump(part[3:4]), -(-rows_x // 8) * 8)
    table_y = tent(part[1:2].astype(I32) + shift_y, bump(part[4:5]), rows_y)
    return table_x, table_y


def run_lists(one, lists, meta, visit):
    def length(dy, dx):
        index = (dy + 1) * 3 + dx + 1
        return meta[index, VISITS + visit] - meta[index, visit]

    most = 0
    for dy, dx, ref in lists:
        one(dy, dx, ref, 0)
        most = jnp.maximum(most, length(dy, dx))

    @pl.when(most > STEP)
    def _():
        for dy, dx, ref in lists:

            def later(step, carry, dy=dy, dx=dx, ref=ref):
                one(dy, dx, ref, step)
                return carry

            steps = lax.shift_right_logical(length(dy, dx) + STEP - 1, 8)
            lax.fori_loop(1, steps, later, 0)


def spread_lists(size_x, size_y, meta, lists, outs, first_row):
    depth = next(iter(outs.values())).shape[3]
    windows = depth // 128
    rows_of = {-1: (0, 5), 0: (2, size_x + 3), 1: (size_x + 2, 4)}

    def clear(e, carry):
        for out_ref in outs.values():
            for c in range(3):
                out_ref[c, e] = jnp.zeros(out_ref.shape[2:], F32)
        return carry

    lax.fori_loop(0, size_x + 2 * HALO, clear, 0)

    def visit_step(visit, carry):
        window = jnp.bitwise_and(visit, windows - 1)
        at = pl.ds(pl.multiple_of(window * 128, 128), 128)

        def one(dy, dx, ref, step):
            out_ref = outs[dy]
            index = (dy + 1) * 3 + dx + 1
            e0, rows = rows_of[dx]
            s0, cols, base = first_row[dy]
            part, _, _, live = markers_of(meta, index, visit, step, ref, dx + 1)
            both = jnp.concatenate(split2(window_of(part, live, window, depth).T), axis=1)
            right = jnp.concatenate([both, both], axis=0)
            table_x, table_y = plane_of(
                part, HALO - 1 + size_x * dx - e0, rows, PAD - 1 + size_y * dy - s0, cols
            )
            for c in range(3):
                pushed = table_y * part[6 + c : 7 + c]
                planar = jnp.concatenate(
                    [table_x[r : r + 1] * pushed for r in range(rows)], axis=0
                )
                sums = nn(jnp.concatenate(split2(planar), axis=1), right)
                sums = sums[:, 0:128] + sums[:, 128:256]
                for r in range(rows):
                    out_ref[c, e0 + r, base : base + cols, at] += sums[r * cols : (r + 1) * cols]

        run_lists(one, lists, meta, visit)
        return carry

    lax.fori_loop(0, windows + 1, visit_step, 0)


ROWS_MID = {0: (PAD - 1, 32, PAD - 1)}
ROWS_SIDE = {-1: (PAD - 3, 8, 0), 1: (32, 8, 0)}


def spread_mid_kernel(size_x, size_y, meta, mid_ref, out_ref):
    lists = [(0, dx, mid_ref) for dx in (0, -1, 1)]
    spread_lists(size_x, size_y, meta, lists, {0: out_ref}, ROWS_MID)


def spread_side_kernel(size_x, size_y, meta, low_ref, high_ref, out_low, out_high):
    lists = [(dy, dx, ref) for dy, ref in ((-1, low_ref), (1, high_ref)) for dx in (0, -1, 1)]
    outs = {-1: out_low, 1: out_high}
    spread_lists(size_x, size_y, meta, lists, outs, ROWS_SIDE)


def spread_mid(meta, mid, size_x, size_y, depth):
    return pl.pallas_call(
        functools.partial(spread_mid_kernel, size_x, size_y),
        out_shape=jax.ShapeDtypeStruct((3, size_x + 2 * HALO, YE, depth), F32),
        in_specs=[smem(), vmem()],
        out_specs=vmem(),
        compiler_params=params(),
        cost_estimate=cost(10**10, 10**7),
        name="spread_mid",
    )(meta, mid)


def spread_side(meta, low, high, size_x, size_y, depth):
    shape = jax.ShapeDtypeStruct((3, size_x + 2 * HALO, 8, depth), F32)
    return pl.pallas_call(
        functools.partial(spread_side_kernel, size_x, size_y),
        out_shape=(shape, shape),
        in_specs=[smem(), vmem(), vmem()],
        out_specs=(vmem(), vmem()),
        compiler_params=params(),
        cost_estimate=cost(10**10, 10**7),
        name="spread_side",
    )(meta, low, high)


def faces_kernel(vel_ref, visc_ref, x_up, x_down, y_up, y_down, x_up_late, x_down_late):
    size_x, size_y = visc_ref.shape[0], visc_ref.shape[1]
    for r in range(X_LAYERS):
        up, down = (x_up, x_down) if r < X_EARLY else (x_up_late, x_down_late)
        at = r if r < X_EARLY else r - X_EARLY
        rows = slice(at * size_y, (at + 1) * size_y)
        c, l = r // HALO, r % HALO
        if c < 3:
            up[rows, :] = vel_ref[c, size_x - HALO + l]
            down[rows, :] = vel_ref[c, l]
        else:
            up[rows, :] = visc_ref[size_x - HALO + 1 + l]
            down[rows, :] = visc_ref[l]
    for x in range(size_x):
        for c in range(3):
            r = (c * size_x + x) * HALO
            y_up[r : r + HALO, :] = vel_ref[c, x, size_y - HALO : size_y, :]
            y_down[r : r + HALO, :] = vel_ref[c, x, 0:HALO, :]
        r = 3 * size_x * HALO + x * (HALO - 1)
        y_up[r : r + HALO - 1, :] = visc_ref[x, size_y - HALO + 1 : size_y, :]
        y_down[r : r + HALO - 1, :] = visc_ref[x, 0 : HALO - 1, :]


def layer_of(early, late, r, size_y):
    if r < X_EARLY:
        return early, r * size_y
    return late, (r - X_EARLY) * size_y


X_LAYERS = 4 * HALO - 1
X_EARLY = 6


def face_rows(size_x, size_y):
    rows_y = 3 * size_x * HALO + size_x * (HALO - 1)
    rows = (X_EARLY * size_y, rows_y, (X_LAYERS - X_EARLY) * size_y)
    return tuple(-(-number // 8) * 8 for number in rows)


def faces(velocity, viscosity):
    size_x, size_y, depth = viscosity.shape
    shapes = [jax.ShapeDtypeStruct((rows, depth), F32) for rows in face_rows(size_x, size_y)]
    return pl.pallas_call(
        faces_kernel,
        out_shape=[shape for shape in shapes for _ in range(2)],
        in_specs=[vmem(), vmem()],
        out_specs=[vmem()] * 6,
        compiler_params=params(),
        cost_estimate=cost(10**6, 10**7),
        name="faces",
    )(velocity, viscosity)


def late_kernel(size_x, up_ref, down_ref, y_low, y_high, up, down):
    thick = up_ref.shape[0]
    up[0:thick, :] = up_ref[...]
    down[0:thick, :] = down_ref[...]
    base = 3 * size_x * HALO
    thin = HALO - 1
    for r in range(X_LAYERS):
        c, l = r // HALO, r % HALO
        for side, ref in ((0, y_low), (1, y_high)):
            for out, x in (
                (up, size_x - HALO + l + (1 if c == 3 else 0)),
                (down, l),
            ):
                at = thick + (r * 2 + side) * HALO
                if c < 3:
                    row = (c * size_x + x) * HALO
                    out[at : at + HALO, :] = ref[row : row + HALO, :]
                else:
                    row = base + x * thin
                    skip = 1 - side
                    out[at + skip : at + skip + thin, :] = ref[row : row + thin, :]


def late_faces(up, down, y_low, y_high, size_x):
    thick = up.shape[0]
    rows = thick + -(-2 * X_LAYERS * HALO // 8) * 8
    shape = jax.ShapeDtypeStruct((rows, up.shape[1]), F32)
    return pl.pallas_call(
        functools.partial(late_kernel, size_x),
        out_shape=(shape, shape),
        in_specs=[vmem()] * 4,
        out_specs=(vmem(), vmem()),
        compiler_params=params(),
        cost_estimate=cost(10**6, 4 * 10**6),
        name="late_faces",
    )(up, down, y_low, y_high)


def solve_kernel(
    sweeps,
    meta,
    spread_ref,
    side_low,
    side_high,
    vel_ref,
    visc_ref,
    x_low,
    x_high,
    x_low_late,
    x_high_late,
    y_low,
    y_high,
    mid_ref,
    low_ref,
    high_ref,
    new_ref,
    part_mid,
    part_low,
    part_high,
    rhs,
    scaled,
    field,
    ratio,
    gathered,
):
    size_x, size_y, depth = visc_ref.shape
    ext = size_x + 2 * HALO
    own = slice(PAD, PAD + size_y)
    below = slice(PAD - HALO, PAD)
    above = slice(PAD + size_y, PAD + size_y + HALO)
    tiles = [slice(s, s + 8) for s in range(0, YE, 8)]
    thick = -(-(X_LAYERS - X_EARLY) * size_y // 8) * 8

    def clear(e, carry):
        for c in range(3):
            rhs[c, e, tiles[0]] = jnp.zeros((8, depth), F32)
            rhs[c, e, tiles[4]] = jnp.zeros((8, depth), F32)
        return carry

    lax.fori_loop(0, ext, clear, 0)

    def clear_ratio(e, carry):
        ratio[e, tiles[0]] = jnp.zeros((8, depth), F32)
        ratio[e, tiles[4]] = jnp.zeros((8, depth), F32)
        return carry

    lax.fori_loop(0, ext - 2, clear_ratio, 0)

    base = 3 * size_x * HALO
    thin = HALO - 1
    for x in range(size_x):
        e = x + HALO - 1
        ratio[e, own, :] = visc_ref[x]
        ratio[e, PAD - thin : PAD, :] = y_low[base + x * thin : base + (x + 1) * thin, :]
        ratio[e, PAD + size_y : PAD + size_y + thin, :] = y_high[
            base + x * thin : base + (x + 1) * thin, :
        ]
        for c in range(3):
            r = (c * size_x + x) * HALO
            rhs[c, x + HALO, own, :] = vel_ref[c, x]
            rhs[c, x + HALO, below, :] = y_low[r : r + HALO, :]
            rhs[c, x + HALO, above, :] = y_high[r : r + HALO, :]
    for side, early, late in ((0, x_low, x_low_late), (1, x_high, x_high_late)):
        for r in range(X_LAYERS):
            c, l = r // HALO, r % HALO
            ref, row = layer_of(early, late, r, size_y)
            at = thick + 2 * r * HALO
            skip = 1 if c == 3 else 0
            if c < 3:
                target = rhs.at[c, l if side == 0 else size_x + HALO + l]
            else:
                target = ratio.at[l if side == 0 else size_x + HALO - 1 + l]
            target[own, :] = ref[row : row + size_y, :]
            target[PAD - HALO + skip : PAD, :] = late[at + skip : at + HALO, :]
            at = at + HALO
            end = HALO - skip
            target[PAD + size_y : PAD + size_y + end, :] = late[at : at + end, :]

    rows8 = iota((8, depth), 0)

    def total(c, e, s):
        value = rhs[c, e, tiles[s], :] + spread_ref[c, e, tiles[s], :]
        if s < 2:
            turned = pltpu.roll(side_low[c, e], PAD - 3, 0)
            keep = rows8 >= PAD - 3 if s == 0 else rows8 < PAD - 3
            value = value + jnp.where(keep, turned, 0.0)
        if s == 4:
            value = value + side_high[c, e]
        return value

    for e in (0, ext - 1):
        for c in range(3):
            for s in range(5):
                rhs[c, e, tiles[s], :] = total(c, e, s)

    def scale(e, carry):
        for s in range(5):
            nu = ratio[e - 1, tiles[s], :]
            inverse = 1.0 / (1.0 + 6.0 * nu)
            ratio[e - 1, tiles[s], :] = nu * inverse
            for c in range(3):
                value = total(c, e, s)
                rhs[c, e, tiles[s], :] = value
                scaled[c, e - 1, tiles[s], :] = value * inverse
        return carry

    lax.fori_loop(1, ext - 1, scale, 0)

    def sweep(source, offset, target, target_offset, first, last, write):
        def row(e, carry):
            for s in range(1 if write else 0, 5):
                factor = ratio[e - 1, tiles[s], :]
                for c in range(3):
                    here = source[c, e - offset, tiles[s], :]
                    beside = source[c, e + 1 - offset, tiles[s], :]
                    beside = beside + source[c, e - 1 - offset, tiles[s], :]
                    if s < 4:
                        beside = beside + source[c, e - offset, s * 8 + 1 : s * 8 + 9, :]
                    else:
                        beside = beside + pltpu.roll(here, 7, 0)
                    if s > 0:
                        beside = beside + source[c, e - offset, s * 8 - 1 : s * 8 + 7, :]
                    else:
                        beside = beside + pltpu.roll(here, 1, 0)
                    beside = beside + pltpu.roll(here, depth - 1, 1) + pltpu.roll(here, 1, 1)
                    value = scaled[c, e - 1, tiles[s], :] + factor * beside
                    if write and s == 4:
                        new_ref[c, e - HALO, 24:size_y, :] = value[0 : size_y - 24]
                        value = jnp.where(rows8 < size_y - 24, value, 0.0)
                    elif write:
                        new_ref[c, e - HALO, (s - 1) * 8 : s * 8, :] = value
                    target[c, e - target_offset, tiles[s], :] = value
            return carry

        lax.fori_loop(first, last, row, 0)

    sweep(rhs, 0, field, 1, 1, ext - 1, False)
    sweep(field, 1, rhs, 0, 2, ext - 2, False)
    sweep(rhs, 0, field, 1, 3, ext - 3, True)

    rows_of = {-1: (0, 2), 0: (0, size_x), 1: (size_x - 1, 1)}
    cols_of = {-1: (8, 8), 0: (8, 32), 1: (32, 8)}
    windows = depth // 128
    gathered[...] = jnp.zeros(gathered.shape, F32)

    def visit_step(visit, carry):
        window = jnp.bitwise_and(visit, windows - 1)
        at = pl.ds(pl.multiple_of(window * 128, 128), 128)

        def one(dy, dx, ref, step):
            index = (dy + 1) * 3 + dx + 1
            e0, rows = rows_of[dx]
            s0, cols = cols_of[dy]
            part, lanes, ahead, live = markers_of(meta, index, visit, step, ref, dx + 1)
            both = jnp.concatenate(split2(window_of(part, live, window, depth)), axis=1)
            right = jnp.concatenate([both, both], axis=0)
            table_x, table_y = plane_of(
                part, size_x * dx - 1 - e0, rows, PAD - 1 + size_y * dy - s0, cols
            )
            found = []
            for c in range(3):
                values = jnp.concatenate(
                    [field[c, e0 + HALO - 1 + r, s0 : s0 + cols, at] for r in range(rows)], axis=0
                )
                sums = nn(jnp.concatenate(split2(values), axis=1), right)
                sums = sums[:, 0:STEP] + sums[:, STEP : 2 * STEP]
                mixed = jnp.zeros((cols, STEP), F32)
                for r in range(rows):
                    mixed = mixed + table_x[r : r + 1] * sums[r * cols : (r + 1) * cols]
                total = jnp.sum(mixed * table_y, axis=0, keepdims=True)
                found.append(jnp.where(live, total, 0.0))
            found = jnp.concatenate([*found, jnp.zeros((5, STEP), F32)], axis=0)
            found = jnp.concatenate([found, jnp.zeros((8, 128), F32)], axis=1)
            gathered[index, :, lanes] += pltpu.roll(found, ahead, 1)

        lists = [
            (dy, dx, ref)
            for dy, ref in ((0, mid_ref), (-1, low_ref), (1, high_ref))
            for dx in (0, -1, 1)
        ]
        run_lists(one, lists, meta, visit)
        return carry

    lax.fori_loop(0, windows + 1, visit_step, 0)
    for dy, part_ref in ((-1, part_low), (0, part_mid), (1, part_high)):
        for dx in range(3):
            part_ref[dx * 3 : dx * 3 + 3, :] = gathered[(dy + 1) * 3 + dx, 0:3, :]


def solve(sweeps, meta, spreads, velocity, viscosity, halos, lists):
    size_x, size_y, depth = viscosity.shape
    ext = size_x + 2 * HALO
    slots = lists[0].shape[2]
    partial = jax.ShapeDtypeStruct((9, slots), F32)
    return pl.pallas_call(
        functools.partial(solve_kernel, sweeps),
        out_shape=(jax.ShapeDtypeStruct(velocity.shape, F32), partial, partial, partial),
        in_specs=[smem()] + [vmem()] * 14,
        out_specs=(vmem(),) * 4,
        scratch_shapes=[
            pltpu.VMEM((3, ext, YE, depth), F32),
            pltpu.VMEM((3, ext - 2, YE, depth), F32),
            pltpu.VMEM((3, ext - 2, YE, depth), F32),
            pltpu.VMEM((ext - 2, YE, depth), F32),
            pltpu.VMEM((9, 8, slots), F32),
        ],
        compiler_params=params(),
        cost_estimate=cost(10**10, 2 * 10**7),
        name="solve",
    )(meta, *spreads, velocity, viscosity, *halos, *lists)


def unsort_kernel(total_ref, rank_ref, out_ref):
    devices = out_ref.shape[0]
    slots = total_ref.shape[1]
    flat = jnp.concatenate([rank_ref[k : k + 1, :] for k in range(CAP)], axis=1)
    block = 256
    sums = jnp.zeros((32, slots), F32)
    for b in range(slots // block):
        values = total_ref[:, b * block : (b + 1) * block]
        parts = jnp.concatenate([*split3(values), jnp.zeros_like(values)], axis=0)
        sums = sums + nn(parts.astype(BF16), place_block(flat, b * block, block))
    rows = sums[0:8] + sums[8:16] + sums[16:24]
    turned = jnp.concatenate(
        [rows[:, k * devices : (k + 1) * devices] for k in range(CAP)], axis=0
    )
    out_ref[...] = turned.T


def unsort(total, rank):
    devices = rank.shape[1]
    return pl.pallas_call(
        unsort_kernel,
        out_shape=jax.ShapeDtypeStruct((devices, CAP * 8), F32),
        in_specs=[vmem(), vmem()],
        out_specs=vmem(),
        compiler_params=params(),
        cost_estimate=cost(10**9, 300_000),
        name="unsort",
    )(total, rank)


def unpack_kernel(owner_ref, rank_ref, back_ref, out_ref):
    markers = owner_ref.shape[1]
    devices = back_ref.shape[0]
    onehot = (iota((devices, markers), 0) == owner_ref[...]).astype(F32).astype(BF16)
    rank = rank_ref[...]
    turned = back_ref[...].T
    picked = None
    for part in split3(turned):
        term = nn(part.astype(BF16), onehot)
        picked = term if picked is None else picked + term
    total = jnp.zeros((8, markers), F32)
    for k in range(CAP):
        total = total + jnp.where(rank == k, picked[k * 8 : (k + 1) * 8], 0.0)
    out_ref[...] = total[0:3]


def unpack(owner_row, rank, back):
    markers = owner_row.shape[1]
    return pl.pallas_call(
        unpack_kernel,
        out_shape=jax.ShapeDtypeStruct((3, markers), F32),
        in_specs=[vmem()] * 3,
        out_specs=vmem(),
        compiler_params=params(),
        cost_estimate=cost(10**8, 100_000),
        name="unpack",
    )(owner_row, rank, back)


def shift_up(x, axis):
    count = lax.axis_size(axis)
    return lax.ppermute(x, axis, [(i, (i + 1) % count) for i in range(count)])


def shift_down(x, axis):
    count = lax.axis_size(axis)
    return lax.ppermute(x, axis, [((i + 1) % count, i) for i in range(count)])


def shards(velocity, viscosity, cells, offsets, forces, owners):
    devices = lax.axis_size("gx") * lax.axis_size("gy")
    size_x, size_y, depth = viscosity.shape
    markers = owners.shape[0]
    owner_row = owners.reshape(1, markers)
    both = ("gx", "gy")

    x_up, x_down, y_up, y_down, x_up_late, x_down_late = faces(velocity, viscosity)
    x_low = shift_up(x_up, "gx")
    x_high = shift_down(x_down, "gx")
    y_low = shift_up(y_up, "gy")
    y_high = shift_down(y_down, "gy")
    owner_row, x_up_late = lax.optimization_barrier((owner_row, x_up_late))
    outgoing, rank = pack(owner_row, cells, offsets, forces, devices)
    received = lax.all_to_all(outgoing, both, split_axis=0, concat_axis=0, tiled=True)
    markers_list, order = sort(received, depth)
    markers_list, x_low, x_high, y_low, y_high = lax.optimization_barrier(
        (markers_list, x_low, x_high, y_low, y_high)
    )
    list_low = shift_up(markers_list, "gx")
    list_high = shift_down(markers_list, "gx")
    x_up_late, x_down_late = late_faces(x_up_late, x_down_late, y_low, y_high, size_x)
    mid = jnp.stack([list_low, markers_list, list_high])
    mid, x_up_late, x_down_late = lax.optimization_barrier((mid, x_up_late, x_down_late))
    x_low_late = shift_up(x_up_late, "gx")
    x_high_late = shift_down(x_down_late, "gx")
    low = shift_up(mid, "gy")
    high = shift_down(mid, "gy")
    halos = (x_low, x_high, x_low_late, x_high_late, y_low, y_high)
    meta_mid = mid[:, 10, 0:64].astype(I32)
    meta_mid = jnp.pad(meta_mid, ((3, 3), (0, 0)))
    spread_own = spread_mid(meta_mid, mid, size_x, size_y, depth)
    low, high, spread_own = lax.optimization_barrier((low, high, spread_own))
    meta = jnp.concatenate([part[:, 10, 0:64] for part in (low, mid, high)], axis=0).astype(I32)
    spreads = (spread_own, *spread_side(meta, low, high, size_x, size_y, depth))
    halos, spreads = lax.optimization_barrier((halos, spreads))
    field, part_mid, part_low, part_high = solve(
        3, meta, spreads, velocity, viscosity, halos, (mid, low, high)
    )
    part = part_mid + shift_down(part_low, "gy") + shift_up(part_high, "gy")
    total = part[3:6] + shift_down(part[0:3], "gx") + shift_up(part[6:9], "gx")
    total = jnp.pad(total, ((0, 5), (0, 0)))
    back = unsort(total, order)
    back = lax.all_to_all(back, both, split_axis=0, concat_axis=0, tiled=True)
    return (field, unpack(owner_row, rank, back))


def solution(mesh):
    in_specs = (
        P(None, "gx", "gy", None),
        P("gx", "gy", None),
        P(None, ("gx", "gy")),
        P(None, ("gx", "gy")),
        P(None, ("gx", "gy")),
        P(("gx", "gy"), None),
    )
    out_specs = (P(None, "gx", "gy", None), P(None, ("gx", "gy")))
    return jax.shard_map(shards, mesh=mesh, in_specs=in_specs, out_specs=out_specs, check_vma=False)
```

profile of v0, /device:TPU:1, one launch (start us, length us, event | category | flops | bytes accessed | tf_op | source)
XLA Modules:
  0.0 204.6 jit_solution(4324292799822994639)
XLA Ops:
  0.6 4.9 %faces.1 = (f32[168,1024]{1,0:T(8,128)}, f32[168,1024]{1,0:T(8,128)}, f32[136,1024]{1,0:T(8,128)}, f32[136,1024]{1,0:T(8,128)}, f32[144,1024]{1,0:T(8,128)}, /*index=5*/f32[144,1024]{1,0:T(8,128)}) custom-call(f32[3,12,28,1024]{3,2,1,0:T(8,128)} %vel_ref.3, f32[12,28,1024]{2,1,0:T(8,128)} %visc_ref.3), custom_call_target="tpu_custom_call" | custom-call | flops 1000000 | bytes 10000000 | tf_op jit(solution)/shard_map/faces/pallas_call | solution.py:408
  5.5 2.5 %collective-permute-start = (f32[168,1024]{1,0:T(8,128)}, f32[168,1024]{1,0:T(8,128)S(1)}, u32[]{:S(2)}, u32[]{:S(2)}) collective-permute-start(f32[168,1024]{1,0:T(8,128)} %get-tuple-element.46), channel_id=1, source_target_pairs={{0,16},{16,32},{32,48},{48,64},{64,80},{80,96},{96,112},{112,0},{1... | collective-permute-start | bytes 2064392 | tf_op jit(solution)/shard_map/ppermute | solution.py:732
  8.0 2.5 %collective-permute-start.1 = (f32[168,1024]{1,0:T(8,128)}, f32[168,1024]{1,0:T(8,128)S(1)}, u32[]{:S(2)}, u32[]{:S(2)}) collective-permute-start(f32[168,1024]{1,0:T(8,128)} %get-tuple-element.47), channel_id=1, source_target_pairs={{16,0},{32,16},{48,32},{64,48},{80,64},{96,80},{112,96},{0,112},{1... | collective-permute-start | bytes 2064392 | tf_op jit(solution)/shard_map/ppermute | solution.py:737
  10.5 2.1 %collective-permute-start.2 = (f32[136,1024]{1,0:T(8,128)}, f32[136,1024]{1,0:T(8,128)S(1)}, u32[]{:S(2)}, u32[]{:S(2)}) collective-permute-start(f32[136,1024]{1,0:T(8,128)} %get-tuple-element.48), channel_id=1, source_target_pairs={{0,1},{1,2},{2,3},{3,4},{4,5},{5,6},{6,7},{7,8},{8,9},{9,10},{10,1... | collective-permute-start | bytes 1671176 | tf_op jit(solution)/shard_map/ppermute | solution.py:732
  12.6 0.0 collective-permute-start.3
  12.6 2.3 %pack.1 = (f32[128,256]{1,0:T(8,128)}, s32[1,1024]{1,0:T(1,128)}) custom-call(s32[1,1024]{1,0:T(1,128)} %bitcast.21, s32[3,1024]{1,0:T(4,128)} %cells_ref.1, f32[3,1024]{1,0:T(4,128)} %offsets_ref.1, f32[3,1024]{1,0:T(4,128)} %forces_ref.1), custom_call_target="tpu_custom_call" | custom-call | flops 400000000 | bytes 300000 | tf_op jit(solution)/shard_map/pack/pallas_call | solution.py:104
  14.8 1.0 copy.13
  15.9 33.7 %all_to_all.22 = f32[128,1,256]{2,1,0:T(1,128)S(1)} all-to-all(f32[128,1,256]{2,1,0:T(1,128)S(1)} %copy.13), channel_id=1, replica_groups=mesh['gx'=8,'gy'=16] {'gx','gy'}, dimensions={0} | all-to-all | bytes 262144 | tf_op jit(solution)/shard_map/all_to_all | solution.py:754
  49.6 0.7 copy.24
  50.3 9.3 %sort.1 = (f32[16,2048]{1,0:T(8,128)}, s32[16,128]{1,0:T(8,128)}) custom-call(f32[128,256]{1,0:T(8,128)} %bitcast.17), custom_call_target="tpu_custom_call" | custom-call | flops 2000000000 | bytes 300000 | tf_op jit(solution)/shard_map/sort/pallas_call | solution.py:198
  59.6 0.0 collective-permute-done.3.y_high
  59.6 0.0 collective-permute-done.1.x_high
  59.7 2.9 %collective-permute-start.5 = (f32[16,2048]{1,0:T(8,128)}, f32[16,2048]{1,0:T(8,128)S(1)}, u32[]{:S(2)}, u32[]{:S(2)}) collective-permute-start(f32[16,2048]{1,0:T(8,128)} %get-tuple-element.50), channel_id=1, source_target_pairs={{16,0},{32,16},{48,32},{64,48},{80,64},{96,80},{112,96},{0,112},{1... | collective-permute-start | bytes 393224 | tf_op jit(solution)/shard_map/ppermute | solution.py:737
  62.6 0.0 collective-permute-start.4
  62.6 1.1 stack.13
  63.7 3.1 %late_faces.1 = (f32[216,1024]{1,0:T(8,128)}, f32[216,1024]{1,0:T(8,128)}) custom-call(f32[144,1024]{1,0:T(8,128)} %get-tuple-element.51.up_ref, f32[144,1024]{1,0:T(8,128)} %get-tuple-element.52.down_ref, f32[136,1024]{1,0:T(8,128)} %copy-done, f32[136,1024]{1,0:T(8,128)} %copy-done.1), custom_call_target="tpu_custom_call" | custom-call | flops 1000000 | bytes 4000000 | tf_op jit(solution)/shard_map/late_faces/pallas_call | solution.py:446
  66.7 0.0 collective-permute-done.5
  66.7 0.1 stack.14
  66.8 2.5 %collective-permute-done.4 = f32[16,2048]{1,0:T(8,128)S(1)} collective-permute-done((f32[16,2048]{1,0:T(8,128)}, f32[16,2048]{1,0:T(8,128)S(1)}, u32[]{:S(2)}, u32[]{:S(2)}) %collective-permute-start.4) | collective-permute-done | bytes 131104 | tf_op jit(solution)/shard_map/ppermute | solution.py:732
  69.3 0.1 stack.12
  69.4 0.3 pad_maximum_fusion
  69.7 0.2 copy.14.mid_ref
  70.0 0.1 collective-permute-start.6
  70.1 1.6 collective-permute-start.7
  71.7 0.0 collective-permute-start.8
  71.7 3.6 %collective-permute-start.9 = (f32[216,1024]{1,0:T(8,128)}, f32[216,1024]{1,0:T(8,128)S(1)}, u32[]{:S(2)}, u32[]{:S(2)}) collective-permute-start(f32[216,1024]{1,0:T(8,128)} %get-tuple-element.63), channel_id=1, source_target_pairs={{16,0},{32,16},{48,32},{64,48},{80,64},{96,80},{112,96},{0,112},{1... | collective-permute-start | bytes 2654216 | tf_op jit(solution)/shard_map/ppermute | solution.py:737
  75.3 0.6 pad.8.meta
  75.9 20.2 %spread_mid.1.spread_ref = f32[3,18,40,1024]{3,2,1,0:T(8,128)} custom-call(s32[9,64]{1,0:T(8,128)} %pad.8.meta, f32[3,16,2048]{2,1,0:T(8,128)} %copy-done.2), custom_call_target="tpu_custom_call" | custom-call | flops 10000000000 | bytes 10000000 | tf_op jit(solution)/shard_map/spread_mid/pallas_call | solution.py:342
  96.1 0.0 collective-permute-done.7.high_ref
  96.1 1.0 copy.16.low_ref
  97.1 0.6 maximum_convert_fusion.meta
  97.7 14.6 %spread_side.1 = (f32[3,18,8,1024]{3,2,1,0:T(8,128)}, f32[3,18,8,1024]{3,2,1,0:T(8,128)}) custom-call(s32[9,64]{1,0:T(8,128)} %maximum_convert_fusion.meta, f32[3,16,2048]{2,1,0:T(8,128)} %copy.16.low_ref, f32[3,16,2048]{2,1,0:T(8,128)} %copy-done.3), custom_call_target="tpu_custom_call" | custom-call | flops 10000000000 | bytes 10000000 | tf_op jit(solution)/shard_map/spread_side/pallas_call | solution.py:355
  112.4 2.2 %collective-permute-done.8.x_low_late = f32[216,1024]{1,0:T(8,128)S(1)} collective-permute-done((f32[216,1024]{1,0:T(8,128)}, f32[216,1024]{1,0:T(8,128)S(1)}, u32[]{:S(2)}, u32[]{:S(2)}) %collective-permute-start.8) | collective-permute-done | bytes 884768 | tf_op jit(solution)/shard_map/ppermute | solution.py:732
  114.6 3.4 %collective-permute-done.9.x_high_late = f32[216,1024]{1,0:T(8,128)S(1)} collective-permute-done((f32[216,1024]{1,0:T(8,128)}, f32[216,1024]{1,0:T(8,128)S(1)}, u32[]{:S(2)}, u32[]{:S(2)}) %collective-permute-start.9) | collective-permute-done | bytes 884768 | tf_op jit(solution)/shard_map/ppermute | solution.py:737
  118.0 0.9 copy-done.5
  118.9 47.0 %solve.1 = (f32[3,12,28,1024]{3,2,1,0:T(8,128)}, f32[9,2048]{1,0:T(8,128)}, f32[9,2048]{1,0:T(8,128)}, f32[9,2048]{1,0:T(8,128)}) custom-call(s32[9,64]{1,0:T(8,128)} %maximum_convert_fusion.meta, f32[3,18,40,1024]{3,2,1,0:T(8,128)} %spread_mid.1.spread_ref, f32[3,18,8,1024]{3,2,1,0:T(8,128)} %get-tuple-element.68.side_low, ...), custom_call_target="tpu_custom_call" | custom-call | flops 10000000000 | bytes 20000000 | tf_op jit(solution)/shard_map/solve/pallas_call | solution.py:653
  165.9 1.1 collective-permute-start.10
  167.0 0.9 collective-permute-start.11
  167.9 2.9 %collective-permute-done.10 = f32[9,2048]{1,0:T(8,128)S(1)} collective-permute-done((f32[9,2048]{1,0:T(8,128)}, f32[9,2048]{1,0:T(8,128)S(1)}, u32[]{:S(2)}, u32[]{:S(2)}) %collective-permute-start.10) | collective-permute-done | bytes 73760 | tf_op jit(solution)/shard_map/ppermute | solution.py:737
  170.7 0.9 add_add_fusion
  171.7 0.1 collective-permute-start.12
  171.8 1.5 collective-permute-start.13
  173.2 1.6 collective-permute-done.12
  174.8 1.9 collective-permute-done.13
  176.7 0.6 pad.9.total_ref
  177.4 3.1 %unsort.1 = f32[128,128]{1,0:T(8,128)} custom-call(f32[8,2048]{1,0:T(8,128)} %pad.9.total_ref, s32[16,128]{1,0:T(8,128)} %get-tuple-element.81.rank_ref), custom_call_target="tpu_custom_call" | custom-call | flops 1000000000 | bytes 300000 | tf_op jit(solution)/shard_map/unsort/pallas_call | solution.py:690
  180.5 22.3 %all_to_all.23 = f32[128,1,128]{2,1,0:T(1,128)} all-to-all(f32[128,1,128]{2,1,0:T(1,128)} %bitcast.20), channel_id=1, replica_groups=mesh['gx'=8,'gy'=16] {'gx','gy'}, dimensions={0} | all-to-all | bytes 131072 | tf_op jit(solution)/shard_map/all_to_all | solution.py:783
  202.7 1.9 unpack.1
  (24 shorter events, 0.1 us)
Async XLA Ops:
  5.5 54.1 %collective-permute-start = (f32[168,1024]{1,0:T(8,128)}, f32[168,1024]{1,0:T(8,128)S(1)}, u32[]{:S(2)}, u32[]{:S(2)}) collective-permute-start(f32[168,1024]{1,0:T(8,128)} %get-tuple-element.46), channel_id=1, source_target_pairs={{0,16},{16,32},{32,48},{48,64},{64,80},{80,96},{96,112},{112,0},{1... | collective-permute-start | bytes 2064392 | tf_op jit(solution)/shard_map/ppermute | solution.py:732
  8.0 51.6 %collective-permute-start.1 = (f32[168,1024]{1,0:T(8,128)}, f32[168,1024]{1,0:T(8,128)S(1)}, u32[]{:S(2)}, u32[]{:S(2)}) collective-permute-start(f32[168,1024]{1,0:T(8,128)} %get-tuple-element.47), channel_id=1, source_target_pairs={{16,0},{32,16},{48,32},{64,48},{80,64},{96,80},{112,96},{0,112},{1... | collective-permute-start | bytes 2064392 | tf_op jit(solution)/shard_map/ppermute | solution.py:737
  10.5 49.1 %collective-permute-start.2 = (f32[136,1024]{1,0:T(8,128)}, f32[136,1024]{1,0:T(8,128)S(1)}, u32[]{:S(2)}, u32[]{:S(2)}) collective-permute-start(f32[136,1024]{1,0:T(8,128)} %get-tuple-element.48), channel_id=1, source_target_pairs={{0,1},{1,2},{2,3},{3,4},{4,5},{5,6},{6,7},{7,8},{8,9},{9,10},{10,1... | collective-permute-start | bytes 1671176 | tf_op jit(solution)/shard_map/ppermute | solution.py:732
  12.6 47.0 %collective-permute-start.3 = (f32[136,1024]{1,0:T(8,128)}, f32[136,1024]{1,0:T(8,128)S(1)}, u32[]{:S(2)}, u32[]{:S(2)}) collective-permute-start(f32[136,1024]{1,0:T(8,128)} %get-tuple-element.49), channel_id=1, source_target_pairs={{1,0},{2,1},{3,2},{4,3},{5,4},{6,5},{7,6},{8,7},{9,8},{10,9},{11,1... | collective-permute-start | bytes 1671176 | tf_op jit(solution)/shard_map/ppermute | solution.py:737
  59.6 4.1 %copy-start = (f32[136,1024]{1,0:T(8,128)}, f32[136,1024]{1,0:T(8,128)S(1)}, u32[]{:S(2)}) copy-start(f32[136,1024]{1,0:T(8,128)S(1)} %collective-permute-done.2.y_low) | copy-start | bytes 1671172
  59.6 4.1 %copy-start.1 = (f32[136,1024]{1,0:T(8,128)}, f32[136,1024]{1,0:T(8,128)S(1)}, u32[]{:S(2)}) copy-start(f32[136,1024]{1,0:T(8,128)S(1)} %collective-permute-done.3.y_high) | copy-start | bytes 1671172
  59.6 3.0 %copy-start.6 = (f32[168,1024]{1,0:T(8,128)}, f32[168,1024]{1,0:T(8,128)S(1)}, u32[]{:S(2)}) copy-start(f32[168,1024]{1,0:T(8,128)S(1)} %collective-permute-done.x_low) | copy-start | bytes 2064388
  59.6 10.4 %copy-start.7 = (f32[168,1024]{1,0:T(8,128)}, f32[168,1024]{1,0:T(8,128)S(1)}, u32[]{:S(2)}) copy-start(f32[168,1024]{1,0:T(8,128)S(1)} %collective-permute-done.1.x_high) | copy-start | bytes 2064388
  59.7 7.1 %collective-permute-start.5 = (f32[16,2048]{1,0:T(8,128)}, f32[16,2048]{1,0:T(8,128)S(1)}, u32[]{:S(2)}, u32[]{:S(2)}) collective-permute-start(f32[16,2048]{1,0:T(8,128)} %get-tuple-element.50), channel_id=1, source_target_pairs={{16,0},{32,16},{48,32},{64,48},{80,64},{96,80},{112,96},{0,112},{1... | collective-permute-start | bytes 393224 | tf_op jit(solution)/shard_map/ppermute | solution.py:737
  62.6 6.7 %collective-permute-start.4 = (f32[16,2048]{1,0:T(8,128)}, f32[16,2048]{1,0:T(8,128)S(1)}, u32[]{:S(2)}, u32[]{:S(2)}) collective-permute-start(f32[16,2048]{1,0:T(8,128)} %get-tuple-element.50), channel_id=1, source_target_pairs={{0,16},{16,32},{32,48},{48,64},{64,80},{80,96},{96,112},{112,0},{1... | collective-permute-start | bytes 393224 | tf_op jit(solution)/shard_map/ppermute | solution.py:732
  70.0 5.9 %copy-start.2 = (f32[3,16,2048]{2,1,0:T(8,128)}, f32[3,16,2048]{2,1,0:T(8,128)S(1)}, u32[]{:S(2)}) copy-start(f32[3,16,2048]{2,1,0:T(8,128)S(1)} %copy.14.mid_ref) | copy-start | bytes 1179652
  70.0 26.1 %collective-permute-start.6 = (f32[3,16,2048]{2,0,1:T(4,128)S(1)}, f32[3,16,2048]{2,0,1:T(4,128)S(1)}, u32[]{:S(2)}, u32[]{:S(2)}) collective-permute-start(f32[3,16,2048]{2,0,1:T(4,128)S(1)} %pad_maximum_fusion), channel_id=1, source_target_pairs={{0,1},{1,2},{2,3},{3,4},{4,5},{5,6},{6,7},{7,8},{8,9},{9,10},{10,1... | collective-permute-start | bytes 1179656 | tf_op jit(solution)/shard_map/ppermute | solution.py:732
  70.1 26.0 %collective-permute-start.7 = (f32[3,16,2048]{2,1,0:T(8,128)S(1)}, f32[3,16,2048]{2,1,0:T(8,128)S(1)}, u32[]{:S(2)}, u32[]{:S(2)}) collective-permute-start(f32[3,16,2048]{2,1,0:T(8,128)S(1)} %copy.14.mid_ref), channel_id=1, source_target_pairs={{1,0},{2,1},{3,2},{4,3},{5,4},{6,5},{7,6},{8,7},{9,8},{10,9},{11,1... | collective-permute-start | bytes 1179656 | tf_op jit(solution)/shard_map/ppermute | solution.py:737
  71.7 42.9 %collective-permute-start.8 = (f32[216,1024]{1,0:T(8,128)}, f32[216,1024]{1,0:T(8,128)S(1)}, u32[]{:S(2)}, u32[]{:S(2)}) collective-permute-start(f32[216,1024]{1,0:T(8,128)} %get-tuple-element.62), channel_id=1, source_target_pairs={{0,16},{16,32},{32,48},{48,64},{64,80},{80,96},{96,112},{112,0},{1... | collective-permute-start | bytes 2654216 | tf_op jit(solution)/shard_map/ppermute | solution.py:732
  71.7 46.3 %collective-permute-start.9 = (f32[216,1024]{1,0:T(8,128)}, f32[216,1024]{1,0:T(8,128)S(1)}, u32[]{:S(2)}, u32[]{:S(2)}) collective-permute-start(f32[216,1024]{1,0:T(8,128)} %get-tuple-element.63), channel_id=1, source_target_pairs={{16,0},{32,16},{48,32},{64,48},{80,64},{96,80},{112,96},{0,112},{1... | collective-permute-start | bytes 2654216 | tf_op jit(solution)/shard_map/ppermute | solution.py:737
  96.1 1.6 copy-start.3
  114.6 3.4 %copy-start.4 = (f32[216,1024]{1,0:T(8,128)}, f32[216,1024]{1,0:T(8,128)S(1)}, u32[]{:S(2)}) copy-start(f32[216,1024]{1,0:T(8,128)S(1)} %collective-permute-done.8.x_low_late) | copy-start | bytes 2654212
  118.0 0.9 copy-start.5
  165.9 4.9 %collective-permute-start.10 = (f32[9,2048]{1,0:T(8,128)}, f32[9,2048]{1,0:T(8,128)S(1)}, u32[]{:S(2)}, u32[]{:S(2)}) collective-permute-start(f32[9,2048]{1,0:T(8,128)} %get-tuple-element.79), channel_id=1, source_target_pairs={{1,0},{2,1},{3,2},{4,3},{5,4},{6,5},{7,6},{8,7},{9,8},{10,9},{11,1... | collective-permute-start | bytes 221192 | tf_op jit(solution)/shard_map/ppermute | solution.py:737
  167.0 3.8 %collective-permute-start.11 = (f32[9,2048]{1,0:T(8,128)}, f32[9,2048]{1,0:T(8,128)S(1)}, u32[]{:S(2)}, u32[]{:S(2)}) collective-permute-start(f32[9,2048]{1,0:T(8,128)} %get-tuple-element.80), channel_id=1, source_target_pairs={{0,1},{1,2},{2,3},{3,4},{4,5},{5,6},{6,7},{7,8},{8,9},{9,10},{10,1... | collective-permute-start | bytes 221192 | tf_op jit(solution)/shard_map/ppermute | solution.py:732
  171.7 3.1 %collective-permute-start.12 = (f32[3,2048]{1,0:T(4,128)S(1)}, f32[3,2048]{1,0:T(4,128)S(1)}, u32[]{:S(2)}, u32[]{:S(2)}) collective-permute-start(f32[3,2048]{1,0:T(4,128)S(1)} %get-tuple-element.84), channel_id=1, source_target_pairs={{16,0},{32,16},{48,32},{64,48},{80,64},{96,80},{112,96},{0,112},{1... | collective-permute-start | bytes 73736 | tf_op jit(solution)/shard_map/ppermute | solution.py:737
  171.8 4.9 %collective-permute-start.13 = (f32[3,2048]{1,0:T(4,128)S(1)}, f32[3,2048]{1,0:T(4,128)S(1)}, u32[]{:S(2)}, u32[]{:S(2)}) collective-permute-start(f32[3,2048]{1,0:T(4,128)S(1)} %get-tuple-element.85), channel_id=1, source_target_pairs={{0,16},{16,32},{32,48},{48,64},{64,80},{80,96},{96,112},{112,0},{1... | collective-permute-start | bytes 73736 | tf_op jit(solution)/shard_map/ppermute | solution.py:732
where the time goes:
time: 206 us; the launch traced here: 205 us
  Pallas kernels  106 us (51%)
  blocking collectives  56 us (27%)
  starting transfers between devices  18.8 us (9%)
  waiting for transfers between devices  14.4 us (7%)
  local copies, waits for them, and re-layouts  6.35 us (3%)
    pallas_call x1, Pallas kernels, solve(): pl.pallas_call(functools.partial(solve_kernel, sweeps), out_shape=(jax.Sh...  47 us
    all_to_all x1, blocking collectives, shards(): lax.all_to_all(outgoing, both, split_axis=0, concat_axis=0, tiled=True)  33.7 us
    all_to_all x1, blocking collectives, shards(): back = lax.all_to_all(back, both, split_axis=0, concat_axis=0, tiled=True)  22.3 us
    pallas_call x1, Pallas kernels, spread_mid(): pl.pallas_call(functools.partial(spread_mid_kernel, size_x, size_y), out_...  20.2 us
    pallas_call x1, Pallas kernels, spread_side(): pl.pallas_call(functools.partial(spread_side_kernel, size_x, size_y), out...  14.6 us
    ppermute x7, starting transfers between devices, shift_down(): return lax.ppermute(x, axis, [((i + 1) % count, i) for i in range(count)])  11.8 us
    pallas_call x1, Pallas kernels, sort(): pl.pallas_call(functools.partial(sort_kernel, depth), out_shape=(jax.Shap...  9.33 us
    ppermute x7, waiting for transfers between devices, shift_down(): return lax.ppermute(x, axis, [((i + 1) % count, i) for i in range(count)])  7.86 us
  transfers between devices with their start and end apart: 14, of which 6 were waited for; matrix products, arithmetic and copies ran while one was open for 2% of the time, Pallas kernels for 24%

commit v1 on v0

--- a/solution.py
+++ b/solution.py
@@ -393,7 +393,7 @@
 
 
 X_LAYERS = 4 * HALO - 1
-X_EARLY = 6
+X_EARLY = 2
 
 
 def face_rows(size_x, size_y):
@@ -414,6 +414,18 @@
         cost_estimate=cost(10**6, 10**7),
         name="faces",
     )(velocity, viscosity)
+
+
+def corner_plan(up):
+    plan, at = [], 0
+    for r in range(X_LAYERS):
+        c, l = r // HALO, r % HALO
+        reach = HALO if c < 3 else HALO - 1
+        away = reach - l if up else l + 1
+        if reach > away:
+            plan.append((r, reach - away, at))
+            at += 2 * (reach - away)
+    return plan, at
 
 
 def late_kernel(size_x, up_ref, down_ref, y_low, y_high, up, down):
@@ -422,26 +434,20 @@
     down[0:thick, :] = down_ref[...]
     base = 3 * size_x * HALO
     thin = HALO - 1
-    for r in range(X_LAYERS):
-        c, l = r // HALO, r % HALO
-        for side, ref in ((0, y_low), (1, y_high)):
-            for out, x in (
-                (up, size_x - HALO + l + (1 if c == 3 else 0)),
-                (down, l),
-            ):
-                at = thick + (r * 2 + side) * HALO
-                if c < 3:
-                    row = (c * size_x + x) * HALO
-                    out[at : at + HALO, :] = ref[row : row + HALO, :]
-                else:
-                    row = base + x * thin
-                    skip = 1 - side
-                    out[at + skip : at + skip + thin, :] = ref[row : row + thin, :]
+    for out, is_up in ((up, True), (down, False)):
+        for r, count, first in corner_plan(is_up)[0]:
+            c, l = r // HALO, r % HALO
+            x = l if not is_up else size_x - HALO + l + (1 if c == 3 else 0)
+            deep, row = (HALO, (c * size_x + x) * HALO) if c < 3 else (thin, base + x * thin)
+            at = thick + first
+            out[at : at + count, :] = y_low[row + deep - count : row + deep, :]
+            at = at + count
+            out[at : at + count, :] = y_high[row : row + count, :]
 
 
 def late_faces(up, down, y_low, y_high, size_x):
     thick = up.shape[0]
-    rows = thick + -(-2 * X_LAYERS * HALO // 8) * 8
+    rows = thick + -(-corner_plan(True)[1] // 8) * 8
     shape = jax.ShapeDtypeStruct((rows, up.shape[1]), F32)
     return pl.pallas_call(
         functools.partial(late_kernel, size_x),
@@ -468,11 +474,9 @@
     x_high_late,
     y_low,
     y_high,
-    mid_ref,
     low_ref,
     high_ref,
     new_ref,
-    part_mid,
     part_low,
     part_high,
     rhs,
@@ -522,17 +526,21 @@
         for r in range(X_LAYERS):
             c, l = r // HALO, r % HALO
             ref, row = layer_of(early, late, r, size_y)
-            at = thick + 2 * r * HALO
-            skip = 1 if c == 3 else 0
             if c < 3:
                 target = rhs.at[c, l if side == 0 else size_x + HALO + l]
             else:
                 target = ratio.at[l if side == 0 else size_x + HALO - 1 + l]
             target[own, :] = ref[row : row + size_y, :]
-            target[PAD - HALO + skip : PAD, :] = late[at + skip : at + HALO, :]
-            at = at + HALO
-            end = HALO - skip
-            target[PAD + size_y : PAD + size_y + end, :] = late[at : at + end, :]
+        for r, count, first in corner_plan(side == 0)[0]:
+            c, l = r // HALO, r % HALO
+            if c < 3:
+                target = rhs.at[c, l if side == 0 else size_x + HALO + l]
+            else:
+                target = ratio.at[l if side == 0 else size_x + HALO - 1 + l]
+            at = thick + first
+            target[PAD - count : PAD, :] = late[at : at + count, :]
+            at = at + count
+            target[PAD + size_y : PAD + size_y + count, :] = late[at : at + count, :]
 
     rows8 = iota((8, depth), 0)
 
@@ -582,24 +590,42 @@
                         beside = beside + pltpu.roll(here, 1, 0)
                     beside = beside + pltpu.roll(here, depth - 1, 1) + pltpu.roll(here, 1, 1)
                     value = scaled[c, e - 1, tiles[s], :] + factor * beside
-                    if write and s == 4:
-                        new_ref[c, e - HALO, 24:size_y, :] = value[0 : size_y - 24]
-                        value = jnp.where(rows8 < size_y - 24, value, 0.0)
-                    elif write:
-                        new_ref[c, e - HALO, (s - 1) * 8 : s * 8, :] = value
-                    target[c, e - target_offset, tiles[s], :] = value
+                    if not write:
+                        target[c, e - target_offset, tiles[s], :] = value
+                    elif s == 4:
+                        target[c, e - target_offset, 24:size_y, :] = value[0 : size_y - 24]
+                    else:
+                        target[c, e - target_offset, (s - 1) * 8 : s * 8, :] = value
             return carry
 
         lax.fori_loop(first, last, row, 0)
 
     sweep(rhs, 0, field, 1, 1, ext - 1, False)
     sweep(field, 1, rhs, 0, 2, ext - 2, False)
-    sweep(rhs, 0, field, 1, 3, ext - 3, True)
-
+    sweep(rhs, 0, new_ref, HALO, 3, ext - 3, True)
+
+    gathered[...] = jnp.zeros(gathered.shape, F32)
+    lists = [(dy, dx, ref) for dy, ref in ((-1, low_ref), (1, high_ref)) for dx in (0, -1, 1)]
+    outs = {(dy, dx): (dy + 1) // 2 * 3 + dx + 1 for dy, dx, _ in lists}
+    sample_lists(meta, lists, new_ref, gathered, outs)
+    for dx in range(3):
+        part_low[dx * 3 : dx * 3 + 3, :] = gathered[dx, 0:3, :]
+        part_high[dx * 3 : dx * 3 + 3, :] = gathered[3 + dx, 0:3, :]
+
+
+def sample_lists(meta, lists, field, out_ref, outs):
+    _, size_x, size_y, depth = field.shape
+    windows = depth // 128
+    whole = size_y // 8 * 8
     rows_of = {-1: (0, 2), 0: (0, size_x), 1: (size_x - 1, 1)}
-    cols_of = {-1: (8, 8), 0: (8, 32), 1: (32, 8)}
-    windows = depth // 128
-    gathered[...] = jnp.zeros(gathered.shape, F32)
+    cols_of = {-1: (0, 8), 0: (0, whole + 8), 1: (whole, 8)}
+
+    def values_of(c, x, dy, at):
+        if dy == -1:
+            return [field[c, x, 0:8, at]]
+        tail = field[c, x, whole:size_y, at]
+        tail = jnp.concatenate([tail, jnp.zeros((whole + 8 - size_y, 128), F32)], axis=0)
+        return [tail] if dy == 1 else [field[c, x, 0:whole, at], tail]
 
     def visit_step(visit, carry):
         window = jnp.bitwise_and(visit, windows - 1)
@@ -607,18 +633,18 @@
 
         def one(dy, dx, ref, step):
             index = (dy + 1) * 3 + dx + 1
-            e0, rows = rows_of[dx]
+            x0, rows = rows_of[dx]
             s0, cols = cols_of[dy]
             part, lanes, ahead, live = markers_of(meta, index, visit, step, ref, dx + 1)
             both = jnp.concatenate(split2(window_of(part, live, window, depth)), axis=1)
             right = jnp.concatenate([both, both], axis=0)
             table_x, table_y = plane_of(
-                part, size_x * dx - 1 - e0, rows, PAD - 1 + size_y * dy - s0, cols
+                part, size_x * dx - 1 - x0, rows, size_y * dy - 1 - s0, cols
             )
             found = []
             for c in range(3):
                 values = jnp.concatenate(
-                    [field[c, e0 + HALO - 1 + r, s0 : s0 + cols, at] for r in range(rows)], axis=0
+                    [v for r in range(rows) for v in values_of(c, x0 + r, dy, at)], axis=0
                 )
                 sums = nn(jnp.concatenate(split2(values), axis=1), right)
                 sums = sums[:, 0:STEP] + sums[:, STEP : 2 * STEP]
@@ -629,20 +655,30 @@
                 found.append(jnp.where(live, total, 0.0))
             found = jnp.concatenate([*found, jnp.zeros((5, STEP), F32)], axis=0)
             found = jnp.concatenate([found, jnp.zeros((8, 128), F32)], axis=1)
-            gathered[index, :, lanes] += pltpu.roll(found, ahead, 1)
-
-        lists = [
-            (dy, dx, ref)
-            for dy, ref in ((0, mid_ref), (-1, low_ref), (1, high_ref))
-            for dx in (0, -1, 1)
-        ]
+            out_ref[outs[dy, dx], :, lanes] += pltpu.roll(found, ahead, 1)
+
         run_lists(one, lists, meta, visit)
         return carry
 
     lax.fori_loop(0, windows + 1, visit_step, 0)
-    for dy, part_ref in ((-1, part_low), (0, part_mid), (1, part_high)):
-        for dx in range(3):
-            part_ref[dx * 3 : dx * 3 + 3, :] = gathered[(dy + 1) * 3 + dx, 0:3, :]
+
+
+def sample_kernel(places, meta, mid_ref, field, out_ref):
+    out_ref[...] = jnp.zeros(out_ref.shape, F32)
+    lists = [(0, dx, mid_ref) for dx in places]
+    sample_lists(meta, lists, field, out_ref, {(0, dx): i for i, dx in enumerate(places)})
+
+
+def sample(meta, mid, field, places):
+    return pl.pallas_call(
+        functools.partial(sample_kernel, places),
+        out_shape=jax.ShapeDtypeStruct((len(places), 8, mid.shape[2]), F32),
+        in_specs=[smem(), vmem(), vmem()],
+        out_specs=vmem(),
+        compiler_params=params(),
+        cost_estimate=cost(5 * 10**9, 5 * 10**6),
+        name="sample",
+    )(meta, mid, field)
 
 
 def solve(sweeps, meta, spreads, velocity, viscosity, halos, lists):
@@ -652,15 +688,15 @@
     partial = jax.ShapeDtypeStruct((9, slots), F32)
     return pl.pallas_call(
         functools.partial(solve_kernel, sweeps),
-        out_shape=(jax.ShapeDtypeStruct(velocity.shape, F32), partial, partial, partial),
-        in_specs=[smem()] + [vmem()] * 14,
-        out_specs=(vmem(),) * 4,
+        out_shape=(jax.ShapeDtypeStruct(velocity.shape, F32), partial, partial),
+        in_specs=[smem()] + [vmem()] * 13,
+        out_specs=(vmem(),) * 3,
         scratch_shapes=[
             pltpu.VMEM((3, ext, YE, depth), F32),
             pltpu.VMEM((3, ext - 2, YE, depth), F32),
             pltpu.VMEM((3, ext - 2, YE, depth), F32),
             pltpu.VMEM((ext - 2, YE, depth), F32),
-            pltpu.VMEM((9, 8, slots), F32),
+            pltpu.VMEM((6, 8, slots), F32),
         ],
         compiler_params=params(),
         cost_estimate=cost(10**10, 2 * 10**7),
@@ -668,14 +704,16 @@
     )(meta, *spreads, velocity, viscosity, *halos, *lists)
 
 
-def unsort_kernel(total_ref, rank_ref, out_ref):
+def unsort_kernel(own_ref, sides_ref, low_ref, high_ref, rank_ref, out_ref):
     devices = out_ref.shape[0]
-    slots = total_ref.shape[1]
+    slots = sides_ref.shape[1]
+    total = own_ref[0, 0:3, :] + sides_ref[3:6, :] + low_ref[...] + high_ref[...]
+    total = jnp.concatenate([total, jnp.zeros((5, slots), F32)], axis=0)
     flat = jnp.concatenate([rank_ref[k : k + 1, :] for k in range(CAP)], axis=1)
     block = 256
     sums = jnp.zeros((32, slots), F32)
     for b in range(slots // block):
-        values = total_ref[:, b * block : (b + 1) * block]
+        values = total[:, b * block : (b + 1) * block]
         parts = jnp.concatenate([*split3(values), jnp.zeros_like(values)], axis=0)
         sums = sums + nn(parts.astype(BF16), place_block(flat, b * block, block))
     rows = sums[0:8] + sums[8:16] + sums[16:24]
@@ -685,17 +723,17 @@
     out_ref[...] = turned.T
 
 
-def unsort(total, rank):
+def unsort(own, sides, low, high, rank):
     devices = rank.shape[1]
     return pl.pallas_call(
         unsort_kernel,
         out_shape=jax.ShapeDtypeStruct((devices, CAP * 8), F32),
-        in_specs=[vmem(), vmem()],
+        in_specs=[vmem()] * 5,
         out_specs=vmem(),
         compiler_params=params(),
         cost_estimate=cost(10**9, 300_000),
         name="unsort",
-    )(total, rank)
+    )(own, sides, low, high, rank)
 
 
 def unpack_kernel(owner_ref, rank_ref, back_ref, out_ref):
@@ -744,14 +782,15 @@
     owner_row = owners.reshape(1, markers)
     both = ("gx", "gy")
 
-    x_up, x_down, y_up, y_down, x_up_late, x_down_late = faces(velocity, viscosity)
+    outgoing, rank = pack(owner_row, cells, offsets, forces, devices)
+    outgoing, face_source = lax.optimization_barrier((outgoing, viscosity))
+    received = lax.all_to_all(outgoing, both, split_axis=0, concat_axis=0, tiled=True)
+    x_up, x_down, y_up, y_down, x_up_late, x_down_late = faces(velocity, face_source)
     x_low = shift_up(x_up, "gx")
     x_high = shift_down(x_down, "gx")
+    received, y_up, y_down = lax.optimization_barrier((received, y_up, y_down))
     y_low = shift_up(y_up, "gy")
     y_high = shift_down(y_down, "gy")
-    owner_row, x_up_late = lax.optimization_barrier((owner_row, x_up_late))
-    outgoing, rank = pack(owner_row, cells, offsets, forces, devices)
-    received = lax.all_to_all(outgoing, both, split_axis=0, concat_axis=0, tiled=True)
     markers_list, order = sort(received, depth)
     markers_list, x_low, x_high, y_low, y_high = lax.optimization_barrier(
         (markers_list, x_low, x_high, y_low, y_high)
@@ -773,13 +812,16 @@
     meta = jnp.concatenate([part[:, 10, 0:64] for part in (low, mid, high)], axis=0).astype(I32)
     spreads = (spread_own, *spread_side(meta, low, high, size_x, size_y, depth))
     halos, spreads = lax.optimization_barrier((halos, spreads))
-    field, part_mid, part_low, part_high = solve(
-        3, meta, spreads, velocity, viscosity, halos, (mid, low, high)
+    field, part_low, part_high = solve(
+        3, meta, spreads, velocity, viscosity, halos, (low, high)
     )
-    part = part_mid + shift_down(part_low, "gy") + shift_up(part_high, "gy")
-    total = part[3:6] + shift_down(part[0:3], "gx") + shift_up(part[6:9], "gx")
-    total = jnp.pad(total, ((0, 5), (0, 0)))
-    back = unsort(total, order)
+    beside = sample(meta, mid, field, (-1, 1))
+    sides = shift_down(part_low, "gy") + shift_up(part_high, "gy")
+    to_low = sides[0:3] + beside[0, 0:3]
+    to_high = sides[6:9] + beside[1, 0:3]
+    to_low, to_high, field_own = lax.optimization_barrier((to_low, to_high, field))
+    own = sample(meta, mid, field_own, (0,))
+    back = unsort(own, sides, shift_down(to_low, "gx"), shift_up(to_high, "gx"), order)
     back = lax.all_to_all(back, both, split_axis=0, concat_axis=0, tiled=True)
     return (field, unpack(owner_row, rank, back))
 

time: 206 us -> 205 us (level)
  blocking collectives: 56 us -> 24.5 us
  waiting for transfers between devices: 14.4 us -> 30 us
  starting transfers between devices: 18.8 us -> 28.8 us
  Pallas kernels: 106 us -> 112 us
    all_to_all x1 -> x0, blocking collectives: 33.7 us -> none  [shards(): lax.all_to_all(outgoing, both, split_axis=0, concat_axis=0, tiled=True)]
    pallas_call x0 -> x2, Pallas kernels: none -> 18.1 us  [sample(): pl.pallas_call(functools.partial(sample_kernel, places), out_shape=jax.Sh...]
    ppermute x7, waiting for transfers between devices: 6.53 us -> 19.3 us  [shift_up(): return lax.ppermute(x, axis, [(i, (i + 1) % count) for i in range(count)])]
    all_to_all x0 -> x1, starting transfers between devices: none -> 11.5 us  [shards(): lax.all_to_all(outgoing, both, split_axis=0, concat_axis=0, tiled=True)]
    pallas_call x1, Pallas kernels: 47 us -> 37.3 us  [solve(): pl.pallas_call(functools.partial(solve_kernel, sweeps), out_shape=(jax.Sh...]
    all_to_all x0 -> x1, waiting for transfers between devices: none -> 5.3 us  [shards(): lax.all_to_all(outgoing, both, split_axis=0, concat_axis=0, tiled=True)]
    pallas_call x1, Pallas kernels: 20.2 us -> 15.6 us  [spread_mid(): pl.pallas_call(functools.partial(spread_mid_kernel, size_x, size_y), out_...]
    ppermute x7, starting transfers between devices: 6.95 us -> 2.84 us  [shift_up(): return lax.ppermute(x, axis, [(i, (i + 1) % count) for i in range(count)])]
  transfers between devices with their start and end apart: 14 -> 15, of which waited for: 6 -> 6; matrix products, arithmetic and copies ran while one was open for 2% -> 2% of each run, Pallas kernels for 24% -> 33%
where the time goes in v1:
time: 205 us; the launch traced here: 204 us
  Pallas kernels  112 us (55%)
  waiting for transfers between devices  30 us (15%)
  starting transfers between devices  28.8 us (14%)
  blocking collectives  24.5 us (12%)
  local copies, waits for them, and re-layouts  5.86 us (3%)
    pallas_call x1, Pallas kernels, solve(): pl.pallas_call(functools.partial(solve_kernel, sweeps), out_shape=(jax.Sh...  37.3 us
    all_to_all x1, blocking collectives, shards(): back = lax.all_to_all(back, both, split_axis=0, concat_axis=0, tiled=True)  24.5 us
    ppermute x7, waiting for transfers between devices, shift_up(): return lax.ppermute(x, axis, [(i, (i + 1) % count) for i in range(count)])  19.3 us
    pallas_call x2, Pallas kernels, sample(): pl.pallas_call(functools.partial(sample_kernel, places), out_shape=jax.Sh...  18.1 us
    pallas_call x1, Pallas kernels, spread_side(): pl.pallas_call(functools.partial(spread_side_kernel, size_x, size_y), out...  16.2 us
    pallas_call x1, Pallas kernels, spread_mid(): pl.pallas_call(functools.partial(spread_mid_kernel, size_x, size_y), out_...  15.6 us
    ppermute x7, starting transfers between devices, shift_down(): return lax.ppermute(x, axis, [((i + 1) % count, i) for i in range(count)])  14.4 us
    all_to_all x1, starting transfers between devices, shards(): lax.all_to_all(outgoing, both, split_axis=0, concat_axis=0, tiled=True)  11.5 us
  transfers between devices with their start and end apart: 15, of which 6 were waited for; matrix products, arithmetic and copies ran while one was open for 2% of the time, Pallas kernels for 33%

profile of v1, /device:TPU:1, one launch (start us, length us, event | category | flops | bytes accessed | tf_op | source)
XLA Modules:
  0.0 203.6 jit_solution(6035550833453554897)
XLA Ops:
  0.6 2.3 %pack.1 = (f32[128,256]{1,0:T(8,128)}, s32[1,1024]{1,0:T(1,128)}) custom-call(s32[1,1024]{1,0:T(1,128)} %bitcast.35, s32[3,1024]{1,0:T(4,128)} %cells_ref.1, f32[3,1024]{1,0:T(4,128)} %offsets_ref.1, f32[3,1024]{1,0:T(4,128)} %forces_ref.1), custom_call_target="tpu_custom_call" | custom-call | flops 400000000 | bytes 300000 | tf_op jit(solution)/shard_map/pack/pallas_call | solution.py:104
  2.9 1.7 copy.14
  4.6 11.5 %all-to-all-start = ((f32[128,1,256]{2,1,0:T(1,128)}), f32[128,1,256]{2,1,0:T(1,128)S(1)}, u32[]{:S(2)}, u32[]{:S(2)}) async-start(f32[128,1,256]{2,1,0:T(1,128)} %copy.14), calls=%async_computation | async-start | bytes 262144 | tf_op jit(solution)/shard_map/all_to_all | solution.py:787
  16.1 4.9 %faces.1 = (f32[56,1024]{1,0:T(8,128)}, f32[56,1024]{1,0:T(8,128)}, f32[136,1024]{1,0:T(8,128)}, f32[136,1024]{1,0:T(8,128)}, f32[256,1024]{1,0:T(8,128)}, /*index=5*/f32[256,1024]{1,0:T(8,128)}) custom-call(f32[3,12,28,1024]{3,2,1,0:T(8,128)} %vel_ref.3, f32[12,28,1024]{2,1,0:T(8,128)} %visc_ref.2), custom_call_target="tpu_custom_call" | custom-call | flops 1000000 | bytes 10000000 | tf_op jit(solution)/shard_map/faces/pallas_call | solution.py:408
  20.9 5.3 %all-to-all-done = f32[128,1,256]{2,1,0:T(1,128)S(1)} async-done(((f32[128,1,256]{2,1,0:T(1,128)}), f32[128,1,256]{2,1,0:T(1,128)S(1)}, u32[]{:S(2)}, u32[]{:S(2)}) %all-to-all-start) | async-done | bytes 131104 | tf_op jit(solution)/shard_map/all_to_all | solution.py:787
  26.2 0.7 copy.28
  26.9 0.6 collective-permute-start.2
  27.5 0.0 collective-permute-start.3
  27.5 0.6 collective-permute-start
  28.1 3.0 %collective-permute-start.1 = (f32[56,1024]{1,0:T(8,128)}, f32[56,1024]{1,0:T(8,128)S(1)}, u32[]{:S(2)}, u32[]{:S(2)}) collective-permute-start(f32[56,1024]{1,0:T(8,128)} %get-tuple-element.55), channel_id=1, source_target_pairs={{16,0},{32,16},{48,32},{64,48},{80,64},{96,80},{112,96},{0,112},{1... | collective-permute-start | bytes 688136 | tf_op jit(solution)/shard_map/ppermute | solution.py:775
  31.1 9.3 %sort.1 = (f32[16,2048]{1,0:T(8,128)}, s32[16,128]{1,0:T(8,128)}) custom-call(f32[128,256]{1,0:T(8,128)} %bitcast.28), custom_call_target="tpu_custom_call" | custom-call | flops 2000000000 | bytes 300000 | tf_op jit(solution)/shard_map/sort/pallas_call | solution.py:198
  40.4 2.2 %collective-permute-done.x_low = f32[56,1024]{1,0:T(8,128)S(1)} collective-permute-done((f32[56,1024]{1,0:T(8,128)}, f32[56,1024]{1,0:T(8,128)S(1)}, u32[]{:S(2)}, u32[]{:S(2)}) %collective-permute-start) | collective-permute-done | bytes 229408 | tf_op jit(solution)/shard_map/ppermute | solution.py:770
  42.6 3.2 %collective-permute-done.1.x_high = f32[56,1024]{1,0:T(8,128)S(1)} collective-permute-done((f32[56,1024]{1,0:T(8,128)}, f32[56,1024]{1,0:T(8,128)S(1)}, u32[]{:S(2)}, u32[]{:S(2)}) %collective-permute-start.1) | collective-permute-done | bytes 229408 | tf_op jit(solution)/shard_map/ppermute | solution.py:775
  45.9 0.0 collective-permute-done.2.y_low
  45.9 1.1 collective-permute-start.5
  47.0 0.4 collective-permute-start.4
  47.4 3.4 %late_faces.1 = (f32[280,1024]{1,0:T(8,128)}, f32[280,1024]{1,0:T(8,128)}) custom-call(f32[256,1024]{1,0:T(8,128)} %get-tuple-element.59.up_ref, f32[256,1024]{1,0:T(8,128)} %get-tuple-element.60.down_ref, f32[136,1024]{1,0:T(8,128)} %copy-done.1, f32[136,1024]{1,0:T(8,128)} %copy-done.2), custom_call_target="tpu_custom_call" | custom-call | flops 1000000 | bytes 4000000 | tf_op jit(solution)/shard_map/late_faces/pallas_call | solution.py:452
  50.9 0.0 collective-permute-done.5
  50.9 2.3 %collective-permute-done.4 = f32[16,2048]{1,0:T(8,128)S(1)} collective-permute-done((f32[16,2048]{1,0:T(8,128)}, f32[16,2048]{1,0:T(8,128)S(1)}, u32[]{:S(2)}, u32[]{:S(2)}) %collective-permute-start.4) | collective-permute-done | bytes 131104 | tf_op jit(solution)/shard_map/ppermute | solution.py:770
  53.2 0.3 copy.15
  53.5 2.3 %collective-permute-start.7 = (f32[3,16,2048]{2,0,1:T(4,128)S(1)}, f32[3,16,2048]{2,0,1:T(4,128)S(1)}, u32[]{:S(2)}, u32[]{:S(2)}) collective-permute-start(f32[3,16,2048]{2,0,1:T(4,128)S(1)} %copy.15), channel_id=1, source_target_pairs={{1,0},{2,1},{3,2},{4,3},{5,4},{6,5},{7,6},{8,7},{9,8},{10,9},{11,1... | collective-permute-start | bytes 1179656 | tf_op jit(solution)/shard_map/ppermute | solution.py:775
  55.8 0.4 collective-permute-start.8
  56.2 3.5 %collective-permute-start.9 = (f32[280,1024]{1,0:T(8,128)}, f32[280,1024]{1,0:T(8,128)}, u32[]{:S(2)}, u32[]{:S(2)}) collective-permute-start(f32[280,1024]{1,0:T(8,128)} %get-tuple-element.71), channel_id=1, source_target_pairs={{16,0},{32,16},{48,32},{64,48},{80,64},{96,80},{112,96},{0,112},{1... | collective-permute-start | bytes 3440648 | tf_op jit(solution)/shard_map/ppermute | solution.py:775
  59.7 0.6 pad.4.meta
  60.3 15.6 %spread_mid.1.spread_ref = f32[3,18,40,1024]{3,2,1,0:T(8,128)} custom-call(s32[9,64]{1,0:T(8,128)} %pad.4.meta, f32[3,16,2048]{2,1,0:T(8,128)} %copy-done), custom_call_target="tpu_custom_call" | custom-call | flops 10000000000 | bytes 10000000 | tf_op jit(solution)/shard_map/spread_mid/pallas_call | solution.py:342
  75.9 0.0 collective-permute-done.7
  76.0 1.0 copy.17.low_ref
  77.0 1.0 copy.18.high_ref
  78.0 0.6 maximum_convert_fusion.meta
  78.6 16.2 %spread_side.1 = (f32[3,18,8,1024]{3,2,1,0:T(8,128)}, f32[3,18,8,1024]{3,2,1,0:T(8,128)}) custom-call(s32[9,64]{1,0:T(8,128)} %maximum_convert_fusion.meta, f32[3,16,2048]{2,1,0:T(8,128)} %copy.17.low_ref, f32[3,16,2048]{2,1,0:T(8,128)} %copy.18.high_ref), custom_call_target="tpu_custom_call" | custom-call | flops 10000000000 | bytes 10000000 | tf_op jit(solution)/shard_map/spread_side/pallas_call | solution.py:355
  94.8 14.8 %collective-permute-done.8.x_low_late = f32[280,1024]{1,0:T(8,128)S(1)} collective-permute-done((f32[280,1024]{1,0:T(8,128)}, f32[280,1024]{1,0:T(8,128)S(1)}, u32[]{:S(2)}, u32[]{:S(2)}) %collective-permute-start.8) | collective-permute-done | bytes 1146912 | tf_op jit(solution)/shard_map/ppermute | solution.py:770
  109.6 2.1 %collective-permute-done.9.x_high_late = f32[280,1024]{1,0:T(8,128)} collective-permute-done((f32[280,1024]{1,0:T(8,128)}, f32[280,1024]{1,0:T(8,128)}, u32[]{:S(2)}, u32[]{:S(2)}) %collective-permute-start.9) | collective-permute-done | bytes 1146912 | tf_op jit(solution)/shard_map/ppermute | solution.py:775
  111.7 37.3 %solve.1 = (f32[3,12,28,1024]{3,2,1,0:T(8,128)}, f32[9,2048]{1,0:T(8,128)}, f32[9,2048]{1,0:T(8,128)}) custom-call(s32[9,64]{1,0:T(8,128)} %maximum_convert_fusion.meta, f32[3,18,40,1024]{3,2,1,0:T(8,128)} %spread_mid.1.spread_ref, f32[3,18,8,1024]{3,2,1,0:T(8,128)} %get-tuple-element.76.side_low, f32[3,18,8,1024]{3,2,1,0:T(8,128)} %get-tuple-element.77.side_high, ...), custom_call_target="tpu_custom_call" | custom-call | flops 10000000000 | bytes 20000000 | tf_op jit(solution)/shard_map/solve/pallas_call | solution.py:689
  149.0 0.8 collective-permute-start.10
  149.8 0.9 collective-permute-start.11
  150.7 8.6 %sample.2 = f32[2,8,2048]{2,1,0:T(8,128)} custom-call(s32[9,64]{1,0:T(8,128)} %maximum_convert_fusion.meta, f32[3,16,2048]{2,1,0:T(8,128)} %copy-done, f32[3,12,28,1024]{3,2,1,0:T(8,128)} %get-tuple-element.88.field), custom_call_target="tpu_custom_call" | custom-call | flops 5000000000 | bytes 5000000 | tf_op jit(solution)/shard_map/sample/pallas_call | solution.py:673
  159.3 0.0 collective-permute-done.10
  159.3 0.0 collective-permute-done.11
  159.4 0.9 fusion
  160.3 3.6 %collective-permute-start.12 = (f32[3,2048]{1,0:T(4,128)S(1)}, f32[3,2048]{1,0:T(4,128)S(1)}, u32[]{:S(2)}, u32[]{:S(2)}) collective-permute-start(f32[3,2048]{1,0:T(4,128)S(1)} %get-tuple-element.89), channel_id=1, source_target_pairs={{16,0},{32,16},{48,32},{64,48},{80,64},{96,80},{112,96},{0,112},{1... | collective-permute-start | bytes 73736 | tf_op jit(solution)/shard_map/ppermute | solution.py:775
  163.9 0.0 collective-permute-start.13
  163.9 9.5 %sample.3.own_ref = f32[1,8,2048]{2,1,0:T(8,128)} custom-call(s32[9,64]{1,0:T(8,128)} %maximum_convert_fusion.meta, f32[3,16,2048]{2,1,0:T(8,128)} %copy-done, f32[3,12,28,1024]{3,2,1,0:T(8,128)} %get-tuple-element.88.field), custom_call_target="tpu_custom_call" | custom-call | flops 5000000000 | bytes 5000000 | tf_op jit(solution)/shard_map/sample/pallas_call | solution.py:673
  173.4 0.0 collective-permute-done.13.high_ref
  173.5 0.6 copy-done.8
  174.0 0.0 copy-done.9
  174.1 3.2 %unsort.1 = f32[128,128]{1,0:T(8,128)} custom-call(f32[1,8,2048]{2,1,0:T(8,128)} %sample.3.own_ref, f32[9,2048]{1,0:T(8,128)} %copy-done.3, f32[3,2048]{1,0:T(4,128)} %copy-done.8, f32[3,2048]{1,0:T(4,128)} %copy-done.9, s32[16,128]{1,0:T(8,128)} %get-tuple-element.91.rank_ref), custom_call_target="tpu_custom_call" | custom-call | flops 1000000000 | bytes 300000 | tf_op jit(solution)/shard_map/unsort/pallas_call | solution.py:728
  177.2 24.5 %all_to_all.23 = f32[128,1,128]{2,1,0:T(1,128)} all-to-all(f32[128,1,128]{2,1,0:T(1,128)} %bitcast.33), channel_id=1, replica_groups=mesh['gx'=8,'gy'=16] {'gx','gy'}, dimensions={0} | all-to-all | bytes 131072 | tf_op jit(solution)/shard_map/all_to_all | solution.py:825
  201.7 1.9 unpack.1
  (27 shorter events, 0.1 us)
Async XLA Ops:
  4.6 21.7 %all-to-all-start = ((f32[128,1,256]{2,1,0:T(1,128)}), f32[128,1,256]{2,1,0:T(1,128)S(1)}, u32[]{:S(2)}, u32[]{:S(2)}) async-start(f32[128,1,256]{2,1,0:T(1,128)} %copy.14), calls=%async_computation | async-start | bytes 262144 | tf_op jit(solution)/shard_map/all_to_all | solution.py:787
  26.9 19.0 %collective-permute-start.2 = (f32[136,1024]{1,0:T(8,128)}, f32[136,1024]{1,0:T(8,128)S(1)}, u32[]{:S(2)}, u32[]{:S(2)}) collective-permute-start(f32[136,1024]{1,0:T(8,128)} %get-tuple-element.56), channel_id=1, source_target_pairs={{0,1},{1,2},{2,3},{3,4},{4,5},{5,6},{6,7},{7,8},{8,9},{9,10},{10,1... | collective-permute-start | bytes 1671176 | tf_op jit(solution)/shard_map/ppermute | solution.py:770
  27.5 18.4 %collective-permute-start.3 = (f32[136,1024]{1,0:T(8,128)}, f32[136,1024]{1,0:T(8,128)S(1)}, u32[]{:S(2)}, u32[]{:S(2)}) collective-permute-start(f32[136,1024]{1,0:T(8,128)} %get-tuple-element.57), channel_id=1, source_target_pairs={{1,0},{2,1},{3,2},{4,3},{5,4},{6,5},{7,6},{8,7},{9,8},{10,9},{11,1... | collective-permute-start | bytes 1671176 | tf_op jit(solution)/shard_map/ppermute | solution.py:775
  27.5 15.1 %collective-permute-start = (f32[56,1024]{1,0:T(8,128)}, f32[56,1024]{1,0:T(8,128)S(1)}, u32[]{:S(2)}, u32[]{:S(2)}) collective-permute-start(f32[56,1024]{1,0:T(8,128)} %get-tuple-element.54), channel_id=1, source_target_pairs={{0,16},{16,32},{32,48},{48,64},{64,80},{80,96},{96,112},{112,0},{1... | collective-permute-start | bytes 688136 | tf_op jit(solution)/shard_map/ppermute | solution.py:770
  28.1 17.8 %collective-permute-start.1 = (f32[56,1024]{1,0:T(8,128)}, f32[56,1024]{1,0:T(8,128)S(1)}, u32[]{:S(2)}, u32[]{:S(2)}) collective-permute-start(f32[56,1024]{1,0:T(8,128)} %get-tuple-element.55), channel_id=1, source_target_pairs={{16,0},{32,16},{48,32},{64,48},{80,64},{96,80},{112,96},{0,112},{1... | collective-permute-start | bytes 688136 | tf_op jit(solution)/shard_map/ppermute | solution.py:775
  40.4 12.8 %copy-start.4 = (f32[16,2048]{1,0:T(8,128)S(1)}, f32[16,2048]{1,0:T(8,128)}, u32[]{:S(2)}) copy-start(f32[16,2048]{1,0:T(8,128)} %get-tuple-element.58) | copy-start | bytes 393220
  42.6 33.3 %copy-start.6 = (f32[56,1024]{1,0:T(8,128)}, f32[56,1024]{1,0:T(8,128)S(1)}, u32[]{:S(2)}) copy-start(f32[56,1024]{1,0:T(8,128)S(1)} %collective-permute-done.x_low) | copy-start | bytes 688132
  45.9 30.1 %copy-start.7 = (f32[56,1024]{1,0:T(8,128)}, f32[56,1024]{1,0:T(8,128)S(1)}, u32[]{:S(2)}) copy-start(f32[56,1024]{1,0:T(8,128)S(1)} %collective-permute-done.1.x_high) | copy-start | bytes 688132
  45.9 1.6 copy-start.1
  45.9 1.6 copy-start.2
  45.9 5.0 %collective-permute-start.5 = (f32[16,2048]{1,0:T(8,128)}, f32[16,2048]{1,0:T(8,128)S(1)}, u32[]{:S(2)}, u32[]{:S(2)}) collective-permute-start(f32[16,2048]{1,0:T(8,128)} %get-tuple-element.58), channel_id=1, source_target_pairs={{16,0},{32,16},{48,32},{64,48},{80,64},{96,80},{112,96},{0,112},{1... | collective-permute-start | bytes 393224 | tf_op jit(solution)/shard_map/ppermute | solution.py:775
  47.0 6.1 %collective-permute-start.4 = (f32[16,2048]{1,0:T(8,128)}, f32[16,2048]{1,0:T(8,128)S(1)}, u32[]{:S(2)}, u32[]{:S(2)}) collective-permute-start(f32[16,2048]{1,0:T(8,128)} %get-tuple-element.58), channel_id=1, source_target_pairs={{0,16},{16,32},{32,48},{48,64},{64,80},{80,96},{96,112},{112,0},{1... | collective-permute-start | bytes 393224 | tf_op jit(solution)/shard_map/ppermute | solution.py:770
  53.2 7.1 %copy-start = (f32[3,16,2048]{2,1,0:T(8,128)}, f32[3,16,2048]{2,1,0:T(8,128)S(1)}, u32[]{:S(2)}) copy-start(f32[3,16,2048]{2,1,0:T(8,128)S(1)} %pad_maximum_fusion.mid_ref) | copy-start | bytes 1179652
  53.5 22.5 %collective-permute-start.7 = (f32[3,16,2048]{2,0,1:T(4,128)S(1)}, f32[3,16,2048]{2,0,1:T(4,128)S(1)}, u32[]{:S(2)}, u32[]{:S(2)}) collective-permute-start(f32[3,16,2048]{2,0,1:T(4,128)S(1)} %copy.15), channel_id=1, source_target_pairs={{1,0},{2,1},{3,2},{4,3},{5,4},{6,5},{7,6},{8,7},{9,8},{10,9},{11,1... | collective-permute-start | bytes 1179656 | tf_op jit(solution)/shard_map/ppermute | solution.py:775
  55.8 20.2 %collective-permute-start.6 = (f32[3,16,2048]{2,0,1:T(4,128)S(1)}, f32[3,16,2048]{2,0,1:T(4,128)S(1)}, u32[]{:S(2)}, u32[]{:S(2)}) collective-permute-start(f32[3,16,2048]{2,0,1:T(4,128)S(1)} %copy.15), channel_id=1, source_target_pairs={{0,1},{1,2},{2,3},{3,4},{4,5},{5,6},{6,7},{7,8},{8,9},{9,10},{10,1... | collective-permute-start | bytes 1179656 | tf_op jit(solution)/shard_map/ppermute | solution.py:770
  55.8 53.8 %collective-permute-start.8 = (f32[280,1024]{1,0:T(8,128)}, f32[280,1024]{1,0:T(8,128)S(1)}, u32[]{:S(2)}, u32[]{:S(2)}) collective-permute-start(f32[280,1024]{1,0:T(8,128)} %get-tuple-element.70), channel_id=1, source_target_pairs={{0,16},{16,32},{32,48},{48,64},{64,80},{80,96},{96,112},{112,0},{1... | collective-permute-start | bytes 3440648 | tf_op jit(solution)/shard_map/ppermute | solution.py:770
  56.2 55.6 %collective-permute-start.9 = (f32[280,1024]{1,0:T(8,128)}, f32[280,1024]{1,0:T(8,128)}, u32[]{:S(2)}, u32[]{:S(2)}) collective-permute-start(f32[280,1024]{1,0:T(8,128)} %get-tuple-element.71), channel_id=1, source_target_pairs={{16,0},{32,16},{48,32},{64,48},{80,64},{96,80},{112,96},{0,112},{1... | collective-permute-start | bytes 3440648 | tf_op jit(solution)/shard_map/ppermute | solution.py:775
  109.6 2.1 %copy-start.5 = (f32[280,1024]{1,0:T(8,128)}, f32[280,1024]{1,0:T(8,128)S(1)}, u32[]{:S(2)}) copy-start(f32[280,1024]{1,0:T(8,128)S(1)} %collective-permute-done.8.x_low_late) | copy-start | bytes 3440644
  149.0 10.3 %collective-permute-start.10 = (f32[9,2048]{1,0:T(8,128)}, f32[9,2048]{1,0:T(8,128)S(1)}, u32[]{:S(2)}, u32[]{:S(2)}) collective-permute-start(f32[9,2048]{1,0:T(8,128)} %get-tuple-element.86), channel_id=1, source_target_pairs={{1,0},{2,1},{3,2},{4,3},{5,4},{6,5},{7,6},{8,7},{9,8},{10,9},{11,1... | collective-permute-start | bytes 221192 | tf_op jit(solution)/shard_map/ppermute | solution.py:775
  149.8 9.5 %collective-permute-start.11 = (f32[9,2048]{1,0:T(8,128)}, f32[9,2048]{1,0:T(8,128)S(1)}, u32[]{:S(2)}, u32[]{:S(2)}) collective-permute-start(f32[9,2048]{1,0:T(8,128)} %get-tuple-element.87), channel_id=1, source_target_pairs={{0,1},{1,2},{2,3},{3,4},{4,5},{5,6},{6,7},{7,8},{8,9},{9,10},{10,1... | collective-permute-start | bytes 221192 | tf_op jit(solution)/shard_map/ppermute | solution.py:770
  159.4 14.1 %copy-start.3 = (f32[9,2048]{1,0:T(8,128)}, f32[9,2048]{1,0:T(8,128)S(1)}, u32[]{:S(2)}) copy-start(f32[9,2048]{1,0:T(8,128)S(1)} %add.11.sides_ref) | copy-start | bytes 221188
  160.3 13.1 %collective-permute-start.12 = (f32[3,2048]{1,0:T(4,128)S(1)}, f32[3,2048]{1,0:T(4,128)S(1)}, u32[]{:S(2)}, u32[]{:S(2)}) collective-permute-start(f32[3,2048]{1,0:T(4,128)S(1)} %get-tuple-element.89), channel_id=1, source_target_pairs={{16,0},{32,16},{48,32},{64,48},{80,64},{96,80},{112,96},{0,112},{1... | collective-permute-start | bytes 73736 | tf_op jit(solution)/shard_map/ppermute | solution.py:775
  163.9 9.5 %collective-permute-start.13 = (f32[3,2048]{1,0:T(4,128)S(1)}, f32[3,2048]{1,0:T(4,128)S(1)}, u32[]{:S(2)}, u32[]{:S(2)}) collective-permute-start(f32[3,2048]{1,0:T(4,128)S(1)} %get-tuple-element.90), channel_id=1, source_target_pairs={{0,16},{16,32},{32,48},{48,64},{64,80},{80,96},{96,112},{112,0},{1... | collective-permute-start | bytes 73736 | tf_op jit(solution)/shard_map/ppermute | solution.py:770
  173.4 0.6 copy-start.8
  173.4 0.6 copy-start.9

commit v2 on v1

--- a/solution.py
+++ b/solution.py
@@ -17,6 +17,8 @@
 YE = 40
 VISITS = 16
 STEP = 256
+GROUP_MID = 3
+GROUP_SIDE = 3
 
 
 def split3(x):
@@ -257,29 +259,40 @@
     return table_x, table_y
 
 
-def run_lists(one, lists, meta, visit):
-    def length(dy, dx):
+def run_visits(one, lists, meta, windows, group):
+    def length(dy, dx, visit):
         index = (dy + 1) * 3 + dx + 1
         return meta[index, VISITS + visit] - meta[index, visit]
 
-    most = 0
-    for dy, dx, ref in lists:
-        one(dy, dx, ref, 0)
-        most = jnp.maximum(most, length(dy, dx))
-
-    @pl.when(most > STEP)
-    def _():
-        for dy, dx, ref in lists:
-
-            def later(step, carry, dy=dy, dx=dx, ref=ref):
-                one(dy, dx, ref, step)
-                return carry
-
-            steps = lax.shift_right_logical(length(dy, dx) + STEP - 1, 8)
-            lax.fori_loop(1, steps, later, 0)
-
-
-def spread_lists(size_x, size_y, meta, lists, outs, first_row):
+    def turn(number, carry):
+        most = 0
+        for g in range(group):
+            visit = number * group + g
+            for dy, dx, ref in lists:
+                one(dy, dx, ref, 0, visit)
+                most = jnp.maximum(most, length(dy, dx, visit))
+
+        @pl.when(most > STEP)
+        def _():
+            def again(visit, inner):
+                for dy, dx, ref in lists:
+
+                    def later(step, kept, dy=dy, dx=dx, ref=ref):
+                        one(dy, dx, ref, step, visit)
+                        return kept
+
+                    steps = lax.shift_right_logical(length(dy, dx, visit) + STEP - 1, 8)
+                    lax.fori_loop(1, steps, later, 0)
+                return inner
+
+            lax.fori_loop(number * group, (number + 1) * group, again, 0)
+
+        return carry
+
+    lax.fori_loop(0, (windows + 1) // group, turn, 0)
+
+
+def spread_lists(size_x, size_y, meta, lists, outs, first_row, group):
     depth = next(iter(outs.values())).shape[3]
     windows = depth // 128
     rows_of = {-1: (0, 5), 0: (2, size_x + 3), 1: (size_x + 2, 4)}
@@ -292,11 +305,9 @@
 
     lax.fori_loop(0, size_x + 2 * HALO, clear, 0)
 
-    def visit_step(visit, carry):
-        window = jnp.bitwise_and(visit, windows - 1)
-        at = pl.ds(pl.multiple_of(window * 128, 128), 128)
-
-        def one(dy, dx, ref, step):
+    def one(dy, dx, ref, step, visit):
+            window = jnp.bitwise_and(visit, windows - 1)
+            at = pl.ds(pl.multiple_of(window * 128, 128), 128)
             out_ref = outs[dy]
             index = (dy + 1) * 3 + dx + 1
             e0, rows = rows_of[dx]
@@ -317,10 +328,7 @@
                 for r in range(rows):
                     out_ref[c, e0 + r, base : base + cols, at] += sums[r * cols : (r + 1) * cols]
 
-        run_lists(one, lists, meta, visit)
-        return carry
-
-    lax.fori_loop(0, windows + 1, visit_step, 0)
+    run_visits(one, lists, meta, windows, group)
 
 
 ROWS_MID = {0: (PAD - 1, 32, PAD - 1)}
@@ -329,13 +337,13 @@
 
 def spread_mid_kernel(size_x, size_y, meta, mid_ref, out_ref):
     lists = [(0, dx, mid_ref) for dx in (0, -1, 1)]
-    spread_lists(size_x, size_y, meta, lists, {0: out_ref}, ROWS_MID)
+    spread_lists(size_x, size_y, meta, lists, {0: out_ref}, ROWS_MID, GROUP_MID)
 
 
 def spread_side_kernel(size_x, size_y, meta, low_ref, high_ref, out_low, out_high):
     lists = [(dy, dx, ref) for dy, ref in ((-1, low_ref), (1, high_ref)) for dx in (0, -1, 1)]
     outs = {-1: out_low, 1: out_high}
-    spread_lists(size_x, size_y, meta, lists, outs, ROWS_SIDE)
+    spread_lists(size_x, size_y, meta, lists, outs, ROWS_SIDE, GROUP_SIDE)
 
 
 def spread_mid(meta, mid, size_x, size_y, depth):
@@ -365,9 +373,9 @@
 
 def faces_kernel(vel_ref, visc_ref, x_up, x_down, y_up, y_down, x_up_late, x_down_late):
     size_x, size_y = visc_ref.shape[0], visc_ref.shape[1]
-    for r in range(X_LAYERS):
+    for r in range(X_FIRST, X_LAYERS):
         up, down = (x_up, x_down) if r < X_EARLY else (x_up_late, x_down_late)
-        at = r if r < X_EARLY else r - X_EARLY
+        at = r - X_FIRST if r < X_EARLY else r - X_EARLY
         rows = slice(at * size_y, (at + 1) * size_y)
         c, l = r // HALO, r % HALO
         if c < 3:
@@ -386,19 +394,21 @@
         y_down[r : r + HALO - 1, :] = visc_ref[x, 0 : HALO - 1, :]
 
 
-def layer_of(early, late, r, size_y):
-    if r < X_EARLY:
-        return early, r * size_y
-    return late, (r - X_EARLY) * size_y
+def layer_of(first, early, late, r, size_y):
+    if r < X_FIRST:
+        return first[r]
+    ref, at = (early, r - X_FIRST) if r < X_EARLY else (late, r - X_EARLY)
+    return ref[at * size_y : (at + 1) * size_y, :]
 
 
 X_LAYERS = 4 * HALO - 1
-X_EARLY = 2
+X_FIRST = 2
+X_EARLY = 5
 
 
 def face_rows(size_x, size_y):
     rows_y = 3 * size_x * HALO + size_x * (HALO - 1)
-    rows = (X_EARLY * size_y, rows_y, (X_LAYERS - X_EARLY) * size_y)
+    rows = ((X_EARLY - X_FIRST) * size_y, rows_y, (X_LAYERS - X_EARLY) * size_y)
     return tuple(-(-number // 8) * 8 for number in rows)
 
 
@@ -468,6 +478,8 @@
     side_high,
     vel_ref,
     visc_ref,
+    x_low_first,
+    x_high_first,
     x_low,
     x_high,
     x_low_late,
@@ -522,15 +534,17 @@
             rhs[c, x + HALO, own, :] = vel_ref[c, x]
             rhs[c, x + HALO, below, :] = y_low[r : r + HALO, :]
             rhs[c, x + HALO, above, :] = y_high[r : r + HALO, :]
-    for side, early, late in ((0, x_low, x_low_late), (1, x_high, x_high_late)):
+    for side, start, early, late in (
+        (0, x_low_first, x_low, x_low_late),
+        (1, x_high_first, x_high, x_high_late),
+    ):
         for r in range(X_LAYERS):
             c, l = r // HALO, r % HALO
-            ref, row = layer_of(early, late, r, size_y)
             if c < 3:
                 target = rhs.at[c, l if side == 0 else size_x + HALO + l]
             else:
                 target = ratio.at[l if side == 0 else size_x + HALO - 1 + l]
-            target[own, :] = ref[row : row + size_y, :]
+            target[own, :] = layer_of(start, early, late, r, size_y)
         for r, count, first in corner_plan(side == 0)[0]:
             c, l = r // HALO, r % HALO
             if c < 3:
@@ -607,13 +621,13 @@
     gathered[...] = jnp.zeros(gathered.shape, F32)
     lists = [(dy, dx, ref) for dy, ref in ((-1, low_ref), (1, high_ref)) for dx in (0, -1, 1)]
     outs = {(dy, dx): (dy + 1) // 2 * 3 + dx + 1 for dy, dx, _ in lists}
-    sample_lists(meta, lists, new_ref, gathered, outs)
+    sample_lists(meta, lists, new_ref, gathered, outs, GROUP_SIDE)
     for dx in range(3):
         part_low[dx * 3 : dx * 3 + 3, :] = gathered[dx, 0:3, :]
         part_high[dx * 3 : dx * 3 + 3, :] = gathered[3 + dx, 0:3, :]
 
 
-def sample_lists(meta, lists, field, out_ref, outs):
+def sample_lists(meta, lists, field, out_ref, outs, group):
     _, size_x, size_y, depth = field.shape
     windows = depth // 128
     whole = size_y // 8 * 8
@@ -627,11 +641,9 @@
         tail = jnp.concatenate([tail, jnp.zeros((whole + 8 - size_y, 128), F32)], axis=0)
         return [tail] if dy == 1 else [field[c, x, 0:whole, at], tail]
 
-    def visit_step(visit, carry):
-        window = jnp.bitwise_and(visit, windows - 1)
-        at = pl.ds(pl.multiple_of(window * 128, 128), 128)
-
-        def one(dy, dx, ref, step):
+    def one(dy, dx, ref, step, visit):
+            window = jnp.bitwise_and(visit, windows - 1)
+            at = pl.ds(pl.multiple_of(window * 128, 128), 128)
             index = (dy + 1) * 3 + dx + 1
             x0, rows = rows_of[dx]
             s0, cols = cols_of[dy]
@@ -657,16 +669,13 @@
             found = jnp.concatenate([found, jnp.zeros((8, 128), F32)], axis=1)
             out_ref[outs[dy, dx], :, lanes] += pltpu.roll(found, ahead, 1)
 
-        run_lists(one, lists, meta, visit)
-        return carry
-
-    lax.fori_loop(0, windows + 1, visit_step, 0)
+    run_visits(one, lists, meta, windows, group)
 
 
 def sample_kernel(places, meta, mid_ref, field, out_ref):
     out_ref[...] = jnp.zeros(out_ref.shape, F32)
     lists = [(0, dx, mid_ref) for dx in places]
-    sample_lists(meta, lists, field, out_ref, {(0, dx): i for i, dx in enumerate(places)})
+    sample_lists(meta, lists, field, out_ref, {(0, dx): i for i, dx in enumerate(places)}, 3)
 
 
 def sample(meta, mid, field, places):
@@ -689,7 +698,7 @@
     return pl.pallas_call(
         functools.partial(solve_kernel, sweeps),
         out_shape=(jax.ShapeDtypeStruct(velocity.shape, F32), partial, partial),
-        in_specs=[smem()] + [vmem()] * 13,
+        in_specs=[smem()] + [vmem()] * 15,
         out_specs=(vmem(),) * 3,
         scratch_shapes=[
             pltpu.VMEM((3, ext, YE, depth), F32),
@@ -782,13 +791,17 @@
     owner_row = owners.reshape(1, markers)
     both = ("gx", "gy")
 
+    x_low_first = shift_up(velocity[0, size_x - HALO : size_x - HALO + X_FIRST], "gx")
+    x_high_first = shift_down(velocity[0, 0:X_FIRST], "gx")
     outgoing, rank = pack(owner_row, cells, offsets, forces, devices)
     outgoing, face_source = lax.optimization_barrier((outgoing, viscosity))
     received = lax.all_to_all(outgoing, both, split_axis=0, concat_axis=0, tiled=True)
     x_up, x_down, y_up, y_down, x_up_late, x_down_late = faces(velocity, face_source)
+    received, x_low_first, x_high_first, x_up, x_down, y_up, y_down = lax.optimization_barrier(
+        (received, x_low_first, x_high_first, x_up, x_down, y_up, y_down)
+    )
     x_low = shift_up(x_up, "gx")
     x_high = shift_down(x_down, "gx")
-    received, y_up, y_down = lax.optimization_barrier((received, y_up, y_down))
     y_low = shift_up(y_up, "gy")
     y_high = shift_down(y_down, "gy")
     markers_list, order = sort(received, depth)
@@ -804,7 +817,7 @@
     x_high_late = shift_down(x_down_late, "gx")
     low = shift_up(mid, "gy")
     high = shift_down(mid, "gy")
-    halos = (x_low, x_high, x_low_late, x_high_late, y_low, y_high)
+    halos = (x_low_first, x_high_first, x_low, x_high, x_low_late, x_high_late, y_low, y_high)
     meta_mid = mid[:, 10, 0:64].astype(I32)
     meta_mid = jnp.pad(meta_mid, ((3, 3), (0, 0)))
     spread_own = spread_mid(meta_mid, mid, size_x, size_y, depth)

time: 205 us -> 197 us (0.961)
  Pallas kernels: 112 us -> 104 us
  waiting for transfers between devices: 30 us -> 22.8 us
  starting transfers between devices: 28.8 us -> 32.6 us
  local copies, waits for them, and re-layouts: 5.86 us -> 8.59 us
    ppermute x7 -> x8, waiting for transfers between devices: 19.3 us -> 12.1 us  [shift_up(): return lax.ppermute(x, axis, [(i, (i + 1) % count) for i in range(count)])]
    ppermute x7 -> x8, starting transfers between devices: 14.4 us -> 20.1 us  [shift_down(): return lax.ppermute(x, axis, [((i + 1) % count, i) for i in range(count)])]
    pallas_call x2, Pallas kernels: 18.1 us -> 14.8 us  [sample(): pl.pallas_call(functools.partial(sample_kernel, places), out_shape=jax.Sh...]
    pallas_call x1, Pallas kernels: 16.2 us -> 14.1 us  [spread_side(): pl.pallas_call(functools.partial(spread_side_kernel, size_x, size_y), out...]
    ppermute x7 -> x8, waiting for transfers between devices: 5.37 us -> 5.27 us  [shift_down(): return lax.ppermute(x, axis, [((i + 1) % count, i) for i in range(count)])]
  transfers between devices with their start and end apart: 15 -> 17, of which waited for: 6 -> 6; matrix products, arithmetic and copies ran while one was open for 2% -> 3% of each run, Pallas kernels for 33% -> 32%
where the time goes in v2:
time: 197 us
  Pallas kernels  104 us (53%)
  starting transfers between devices  32.6 us (17%)
  blocking collectives  25.7 us (13%)
  waiting for transfers between devices  22.8 us (12%)
  local copies, waits for them, and re-layouts  8.59 us (4%)
  other arithmetic  2.49 us (1%)
    pallas_call x1, Pallas kernels, solve(): pl.pallas_call(functools.partial(solve_kernel, sweeps), out_shape=(jax.Sh...  35.3 us
    all_to_all x1, blocking collectives, shards(): back = lax.all_to_all(back, both, split_axis=0, concat_axis=0, tiled=True)  25.7 us
    ppermute x8, starting transfers between devices, shift_down(): return lax.ppermute(x, axis, [((i + 1) % count, i) for i in range(count)])  20.1 us
    pallas_call x1, Pallas kernels, spread_mid(): pl.pallas_call(functools.partial(spread_mid_kernel, size_x, size_y), out_...  15.7 us
    pallas_call x2, Pallas kernels, sample(): pl.pallas_call(functools.partial(sample_kernel, places), out_shape=jax.Sh...  14.8 us
    pallas_call x1, Pallas kernels, spread_side(): pl.pallas_call(functools.partial(spread_side_kernel, size_x, size_y), out...  14.1 us
    ppermute x8, waiting for transfers between devices, shift_up(): return lax.ppermute(x, axis, [(i, (i + 1) % count) for i in range(count)])  12.1 us
    all_to_all x1, starting transfers between devices, shards(): lax.all_to_all(outgoing, both, split_axis=0, concat_axis=0, tiled=True)  10.5 us
  transfers between devices with their start and end apart: 17, of which 6 were waited for; matrix products, arithmetic and copies ran while one was open for 3% of the time, Pallas kernels for 32%

profile of v2, /device:TPU:1, one launch (start us, length us, event | category | flops | bytes accessed | tf_op | source)
XLA Modules:
  0.0 197.2 jit_solution(14565314324018075617)
XLA Ops:
  0.6 1.1 slice_bitcast_fusion
  1.7 5.0 %collective-permute-start.1 = (f32[2,28,1024]{2,1,0:T(8,128)S(1)}, f32[2,28,1024]{2,1,0:T(8,128)S(1)}, u32[]{:S(2)}, u32[]{:S(2)}) collective-permute-start(f32[2,28,1024]{2,1,0:T(8,128)S(1)} %get-tuple-element.104), channel_id=1, source_target_pairs={{16,0},{32,16},{48,32},{64,48},{80,64},{96,80},{112,96},{0,112},{1... | collective-permute-start | bytes 688136 | tf_op jit(solution)/shard_map/ppermute | solution.py:784
  6.7 2.3 %pack.1 = (f32[128,256]{1,0:T(8,128)}, s32[1,1024]{1,0:T(1,128)}) custom-call(s32[1,1024]{1,0:T(1,128)} %bitcast.39, s32[3,1024]{1,0:T(4,128)} %cells_ref.1, f32[3,1024]{1,0:T(4,128)} %offsets_ref.1, f32[3,1024]{1,0:T(4,128)} %forces_ref.1), custom_call_target="tpu_custom_call" | custom-call | flops 400000000 | bytes 300000 | tf_op jit(solution)/shard_map/pack/pallas_call | solution.py:106
  8.9 1.7 copy.14
  10.6 10.5 %all-to-all-start = ((f32[128,1,256]{2,1,0:T(1,128)}), f32[128,1,256]{2,1,0:T(1,128)S(1)}, u32[]{:S(2)}, u32[]{:S(2)}) async-start(f32[128,1,256]{2,1,0:T(1,128)} %copy.14), calls=%async_computation | async-start | bytes 262144 | tf_op jit(solution)/shard_map/all_to_all | solution.py:798
  21.2 4.8 %faces.1 = (f32[88,1024]{1,0:T(8,128)}, f32[88,1024]{1,0:T(8,128)}, f32[136,1024]{1,0:T(8,128)}, f32[136,1024]{1,0:T(8,128)}, f32[168,1024]{1,0:T(8,128)}, /*index=5*/f32[168,1024]{1,0:T(8,128)}) custom-call(f32[3,12,28,1024]{3,2,1,0:T(8,128)} %vel_ref.3, f32[12,28,1024]{2,1,0:T(8,128)} %visc_ref.2), custom_call_target="tpu_custom_call" | custom-call | flops 1000000 | bytes 10000000 | tf_op jit(solution)/shard_map/faces/pallas_call | solution.py:418
  25.9 5.4 %all-to-all-done = f32[128,1,256]{2,1,0:T(1,128)S(1)} async-done(((f32[128,1,256]{2,1,0:T(1,128)}), f32[128,1,256]{2,1,0:T(1,128)S(1)}, u32[]{:S(2)}, u32[]{:S(2)}) %all-to-all-start) | async-done | bytes 131104 | tf_op jit(solution)/shard_map/all_to_all | solution.py:798
  31.3 0.7 copy.28
  32.0 0.7 copy-done.8
  32.7 0.1 copy-done.9
  32.8 0.6 collective-permute-start.4
  33.4 0.0 collective-permute-start.5
  33.4 0.6 collective-permute-start.2
  33.9 3.0 %collective-permute-start.3 = (f32[88,1024]{1,0:T(8,128)}, f32[88,1024]{1,0:T(8,128)S(1)}, u32[]{:S(2)}, u32[]{:S(2)}) collective-permute-start(f32[88,1024]{1,0:T(8,128)} %get-tuple-element.63), channel_id=1, source_target_pairs={{16,0},{32,16},{48,32},{64,48},{80,64},{96,80},{112,96},{0,112},{1... | collective-permute-start | bytes 1081352 | tf_op jit(solution)/shard_map/ppermute | solution.py:784
  37.0 9.3 %sort.1 = (f32[16,2048]{1,0:T(8,128)}, s32[16,128]{1,0:T(8,128)}) custom-call(f32[128,256]{1,0:T(8,128)} %bitcast.32), custom_call_target="tpu_custom_call" | custom-call | flops 2000000000 | bytes 300000 | tf_op jit(solution)/shard_map/sort/pallas_call | solution.py:200
  46.3 7.8 %collective-permute-done.2.x_low = f32[88,1024]{1,0:T(8,128)S(1)} collective-permute-done((f32[88,1024]{1,0:T(8,128)}, f32[88,1024]{1,0:T(8,128)S(1)}, u32[]{:S(2)}, u32[]{:S(2)}) %collective-permute-start.2) | collective-permute-done | bytes 360480 | tf_op jit(solution)/shard_map/ppermute | solution.py:779
  54.1 3.2 %collective-permute-done.3.x_high = f32[88,1024]{1,0:T(8,128)S(1)} collective-permute-done((f32[88,1024]{1,0:T(8,128)}, f32[88,1024]{1,0:T(8,128)S(1)}, u32[]{:S(2)}, u32[]{:S(2)}) %collective-permute-start.3) | collective-permute-done | bytes 360480 | tf_op jit(solution)/shard_map/ppermute | solution.py:784
  57.4 0.0 collective-permute-done.4.y_low
  57.4 1.1 collective-permute-start.7
  58.5 0.4 collective-permute-start.6
  59.0 2.9 %late_faces.1 = (f32[192,1024]{1,0:T(8,128)}, f32[192,1024]{1,0:T(8,128)}) custom-call(f32[168,1024]{1,0:T(8,128)} %get-tuple-element.67.up_ref, f32[168,1024]{1,0:T(8,128)} %get-tuple-element.68.down_ref, f32[136,1024]{1,0:T(8,128)} %copy-done.1, f32[136,1024]{1,0:T(8,128)} %copy-done.2), custom_call_target="tpu_custom_call" | custom-call | flops 1000000 | bytes 4000000 | tf_op jit(solution)/shard_map/late_faces/pallas_call | solution.py:462
  61.9 0.0 collective-permute-done.7
  61.9 2.8 %collective-permute-done.6 = f32[16,2048]{1,0:T(8,128)S(1)} collective-permute-done((f32[16,2048]{1,0:T(8,128)}, f32[16,2048]{1,0:T(8,128)S(1)}, u32[]{:S(2)}, u32[]{:S(2)}) %collective-permute-start.6) | collective-permute-done | bytes 131104 | tf_op jit(solution)/shard_map/ppermute | solution.py:779
  64.7 0.9 pad_maximum_fusion.mid_ref
  65.6 0.3 copy.15
  65.9 2.3 %collective-permute-start.9 = (f32[3,16,2048]{2,0,1:T(4,128)S(1)}, f32[3,16,2048]{2,0,1:T(4,128)S(1)}, u32[]{:S(2)}, u32[]{:S(2)}) collective-permute-start(f32[3,16,2048]{2,0,1:T(4,128)S(1)} %copy.15), channel_id=1, source_target_pairs={{1,0},{2,1},{3,2},{4,3},{5,4},{6,5},{7,6},{8,7},{9,8},{10,9},{11,1... | collective-permute-start | bytes 1179656 | tf_op jit(solution)/shard_map/ppermute | solution.py:784
  68.2 0.4 collective-permute-start.10
  68.6 3.5 %collective-permute-start.11 = (f32[192,1024]{1,0:T(8,128)}, f32[192,1024]{1,0:T(8,128)S(1)}, u32[]{:S(2)}, u32[]{:S(2)}) collective-permute-start(f32[192,1024]{1,0:T(8,128)} %get-tuple-element.81), channel_id=1, source_target_pairs={{16,0},{32,16},{48,32},{64,48},{80,64},{96,80},{112,96},{0,112},{1... | collective-permute-start | bytes 2359304 | tf_op jit(solution)/shard_map/ppermute | solution.py:784
  72.1 0.6 pad.4.meta
  72.7 15.7 %spread_mid.1.spread_ref = f32[3,18,40,1024]{3,2,1,0:T(8,128)} custom-call(s32[9,64]{1,0:T(8,128)} %pad.4.meta, f32[3,16,2048]{2,1,0:T(8,128)} %copy-done), custom_call_target="tpu_custom_call" | custom-call | flops 10000000000 | bytes 10000000 | tf_op jit(solution)/shard_map/spread_mid/pallas_call | solution.py:350
  88.4 1.0 copy.17.low_ref
  89.4 1.0 copy.18.high_ref
  90.4 0.6 maximum_convert_fusion.meta
  91.0 14.1 %spread_side.1 = (f32[3,18,8,1024]{3,2,1,0:T(8,128)}, f32[3,18,8,1024]{3,2,1,0:T(8,128)}) custom-call(s32[9,64]{1,0:T(8,128)} %maximum_convert_fusion.meta, f32[3,16,2048]{2,1,0:T(8,128)} %copy.17.low_ref, f32[3,16,2048]{2,1,0:T(8,128)} %copy.18.high_ref), custom_call_target="tpu_custom_call" | custom-call | flops 10000000000 | bytes 10000000 | tf_op jit(solution)/shard_map/spread_side/pallas_call | solution.py:363
  105.1 1.5 collective-permute-done.10.x_low_late
  106.6 2.0 %collective-permute-done.11.x_high_late = f32[192,1024]{1,0:T(8,128)S(1)} collective-permute-done((f32[192,1024]{1,0:T(8,128)}, f32[192,1024]{1,0:T(8,128)S(1)}, u32[]{:S(2)}, u32[]{:S(2)}) %collective-permute-start.11) | collective-permute-done | bytes 786464 | tf_op jit(solution)/shard_map/ppermute | solution.py:784
  108.6 0.9 copy-done.5
  109.5 35.3 %solve.1 = (f32[3,12,28,1024]{3,2,1,0:T(8,128)}, f32[9,2048]{1,0:T(8,128)}, f32[9,2048]{1,0:T(8,128)}) custom-call(s32[9,64]{1,0:T(8,128)} %maximum_convert_fusion.meta, f32[3,18,40,1024]{3,2,1,0:T(8,128)} %spread_mid.1.spread_ref, f32[3,18,8,1024]{3,2,1,0:T(8,128)} %get-tuple-element.86.side_low, f32[3,18,8,1024]{3,2,1,0:T(8,128)} %get-tuple-element.87.side_high, ...), custom_call_target="tpu_custom_call" | custom-call | flops 10000000000 | bytes 20000000 | tf_op jit(solution)/shard_map/solve/pallas_call | solution.py:698
  144.8 2.9 %collective-permute-start.12 = (f32[9,2048]{1,0:T(8,128)}, f32[9,2048]{1,0:T(8,128)S(1)}, u32[]{:S(2)}, u32[]{:S(2)}) collective-permute-start(f32[9,2048]{1,0:T(8,128)} %get-tuple-element.98), channel_id=1, source_target_pairs={{1,0},{2,1},{3,2},{4,3},{5,4},{6,5},{7,6},{8,7},{9,8},{10,9},{11,1... | collective-permute-start | bytes 221192 | tf_op jit(solution)/shard_map/ppermute | solution.py:784
  147.7 7.6 %sample.2 = f32[2,8,2048]{2,1,0:T(8,128)} custom-call(s32[9,64]{1,0:T(8,128)} %maximum_convert_fusion.meta, f32[3,16,2048]{2,1,0:T(8,128)} %copy-done, f32[3,12,28,1024]{3,2,1,0:T(8,128)} %get-tuple-element.100.field), custom_call_target="tpu_custom_call" | custom-call | flops 5000000000 | bytes 5000000 | tf_op jit(solution)/shard_map/sample/pallas_call | solution.py:682
  155.4 0.9 fusion
  156.3 2.3 %collective-permute-start.14 = (f32[3,2048]{1,0:T(4,128)S(1)}, f32[3,2048]{1,0:T(4,128)S(1)}, u32[]{:S(2)}, u32[]{:S(2)}) collective-permute-start(f32[3,2048]{1,0:T(4,128)S(1)} %get-tuple-element.101), channel_id=1, source_target_pairs={{16,0},{32,16},{48,32},{64,48},{80,64},{96,80},{112,96},{0,112},{1... | collective-permute-start | bytes 73736 | tf_op jit(solution)/shard_map/ppermute | solution.py:784
  158.6 7.2 %sample.3.own_ref = f32[1,8,2048]{2,1,0:T(8,128)} custom-call(s32[9,64]{1,0:T(8,128)} %maximum_convert_fusion.meta, f32[3,16,2048]{2,1,0:T(8,128)} %copy-done, f32[3,12,28,1024]{3,2,1,0:T(8,128)} %get-tuple-element.100.field), custom_call_target="tpu_custom_call" | custom-call | flops 5000000000 | bytes 5000000 | tf_op jit(solution)/shard_map/sample/pallas_call | solution.py:682
  165.8 0.6 copy-done.10
  166.4 0.0 copy-done.11
  166.4 3.2 %unsort.1 = f32[128,128]{1,0:T(8,128)} custom-call(f32[1,8,2048]{2,1,0:T(8,128)} %sample.3.own_ref, f32[9,2048]{1,0:T(8,128)} %copy-done.3, f32[3,2048]{1,0:T(4,128)} %copy-done.10, f32[3,2048]{1,0:T(4,128)} %copy-done.11, s32[16,128]{1,0:T(8,128)} %get-tuple-element.103.rank_ref), custom_call_target="tpu_custom_call" | custom-call | flops 1000000000 | bytes 300000 | tf_op jit(solution)/shard_map/unsort/pallas_call | solution.py:737
  169.6 25.7 %all_to_all.23 = f32[128,1,128]{2,1,0:T(1,128)} all-to-all(f32[128,1,128]{2,1,0:T(1,128)} %bitcast.37), channel_id=1, replica_groups=mesh['gx'=8,'gy'=16] {'gx','gy'}, dimensions={0} | all-to-all | bytes 131072 | tf_op jit(solution)/shard_map/all_to_all | solution.py:838
  195.3 1.9 unpack.1
  (36 shorter events, 0.1 us)
Async XLA Ops:
  1.7 30.3 %collective-permute-start.1 = (f32[2,28,1024]{2,1,0:T(8,128)S(1)}, f32[2,28,1024]{2,1,0:T(8,128)S(1)}, u32[]{:S(2)}, u32[]{:S(2)}) collective-permute-start(f32[2,28,1024]{2,1,0:T(8,128)S(1)} %get-tuple-element.104), channel_id=1, source_target_pairs={{16,0},{32,16},{48,32},{64,48},{80,64},{96,80},{112,96},{0,112},{1... | collective-permute-start | bytes 688136 | tf_op jit(solution)/shard_map/ppermute | solution.py:784
  6.7 25.3 %collective-permute-start = (f32[2,28,1024]{2,1,0:T(8,128)S(1)}, f32[2,28,1024]{2,1,0:T(8,128)S(1)}, u32[]{:S(2)}, u32[]{:S(2)}) collective-permute-start(f32[2,28,1024]{2,1,0:T(8,128)S(1)} %get-tuple-element.105), channel_id=1, source_target_pairs={{0,16},{16,32},{32,48},{48,64},{64,80},{80,96},{96,112},{112,0},{1... | collective-permute-start | bytes 688136 | tf_op jit(solution)/shard_map/ppermute | solution.py:779
  10.6 20.7 %all-to-all-start = ((f32[128,1,256]{2,1,0:T(1,128)}), f32[128,1,256]{2,1,0:T(1,128)S(1)}, u32[]{:S(2)}, u32[]{:S(2)}) async-start(f32[128,1,256]{2,1,0:T(1,128)} %copy.14), calls=%async_computation | async-start | bytes 262144 | tf_op jit(solution)/shard_map/all_to_all | solution.py:798
  32.0 0.7 copy-start.8
  32.0 0.8 copy-start.9
  32.8 24.6 %collective-permute-start.4 = (f32[136,1024]{1,0:T(8,128)}, f32[136,1024]{1,0:T(8,128)S(1)}, u32[]{:S(2)}, u32[]{:S(2)}) collective-permute-start(f32[136,1024]{1,0:T(8,128)} %get-tuple-element.64), channel_id=1, source_target_pairs={{0,1},{1,2},{2,3},{3,4},{4,5},{5,6},{6,7},{7,8},{8,9},{9,10},{10,1... | collective-permute-start | bytes 1671176 | tf_op jit(solution)/shard_map/ppermute | solution.py:779
  33.4 24.0 %collective-permute-start.5 = (f32[136,1024]{1,0:T(8,128)}, f32[136,1024]{1,0:T(8,128)S(1)}, u32[]{:S(2)}, u32[]{:S(2)}) collective-permute-start(f32[136,1024]{1,0:T(8,128)} %get-tuple-element.65), channel_id=1, source_target_pairs={{1,0},{2,1},{3,2},{4,3},{5,4},{6,5},{7,6},{8,7},{9,8},{10,9},{11,1... | collective-permute-start | bytes 1671176 | tf_op jit(solution)/shard_map/ppermute | solution.py:784
  33.4 20.8 %collective-permute-start.2 = (f32[88,1024]{1,0:T(8,128)}, f32[88,1024]{1,0:T(8,128)S(1)}, u32[]{:S(2)}, u32[]{:S(2)}) collective-permute-start(f32[88,1024]{1,0:T(8,128)} %get-tuple-element.62), channel_id=1, source_target_pairs={{0,16},{16,32},{32,48},{48,64},{64,80},{80,96},{96,112},{112,0},{1... | collective-permute-start | bytes 1081352 | tf_op jit(solution)/shard_map/ppermute | solution.py:779
  33.9 23.4 %collective-permute-start.3 = (f32[88,1024]{1,0:T(8,128)}, f32[88,1024]{1,0:T(8,128)S(1)}, u32[]{:S(2)}, u32[]{:S(2)}) collective-permute-start(f32[88,1024]{1,0:T(8,128)} %get-tuple-element.63), channel_id=1, source_target_pairs={{16,0},{32,16},{48,32},{64,48},{80,64},{96,80},{112,96},{0,112},{1... | collective-permute-start | bytes 1081352 | tf_op jit(solution)/shard_map/ppermute | solution.py:784
  54.1 34.2 %copy-start.6 = (f32[88,1024]{1,0:T(8,128)}, f32[88,1024]{1,0:T(8,128)S(1)}, u32[]{:S(2)}) copy-start(f32[88,1024]{1,0:T(8,128)S(1)} %collective-permute-done.2.x_low) | copy-start | bytes 1081348
  57.4 7.3 %copy-start.7 = (f32[88,1024]{1,0:T(8,128)}, f32[88,1024]{1,0:T(8,128)S(1)}, u32[]{:S(2)}) copy-start(f32[88,1024]{1,0:T(8,128)S(1)} %collective-permute-done.3.x_high) | copy-start | bytes 1081348
  57.4 1.6 copy-start.1
  57.4 1.6 copy-start.2
  57.4 4.5 %collective-permute-start.7 = (f32[16,2048]{1,0:T(8,128)}, f32[16,2048]{1,0:T(8,128)S(1)}, u32[]{:S(2)}, u32[]{:S(2)}) collective-permute-start(f32[16,2048]{1,0:T(8,128)} %get-tuple-element.66), channel_id=1, source_target_pairs={{16,0},{32,16},{48,32},{64,48},{80,64},{96,80},{112,96},{0,112},{1... | collective-permute-start | bytes 393224 | tf_op jit(solution)/shard_map/ppermute | solution.py:784
  58.5 6.1 %collective-permute-start.6 = (f32[16,2048]{1,0:T(8,128)}, f32[16,2048]{1,0:T(8,128)S(1)}, u32[]{:S(2)}, u32[]{:S(2)}) collective-permute-start(f32[16,2048]{1,0:T(8,128)} %get-tuple-element.66), channel_id=1, source_target_pairs={{0,16},{16,32},{32,48},{48,64},{64,80},{80,96},{96,112},{112,0},{1... | collective-permute-start | bytes 393224 | tf_op jit(solution)/shard_map/ppermute | solution.py:779
  65.6 7.1 %copy-start = (f32[3,16,2048]{2,1,0:T(8,128)}, f32[3,16,2048]{2,1,0:T(8,128)S(1)}, u32[]{:S(2)}) copy-start(f32[3,16,2048]{2,1,0:T(8,128)S(1)} %pad_maximum_fusion.mid_ref) | copy-start | bytes 1179652
  65.9 22.5 %collective-permute-start.9 = (f32[3,16,2048]{2,0,1:T(4,128)S(1)}, f32[3,16,2048]{2,0,1:T(4,128)S(1)}, u32[]{:S(2)}, u32[]{:S(2)}) collective-permute-start(f32[3,16,2048]{2,0,1:T(4,128)S(1)} %copy.15), channel_id=1, source_target_pairs={{1,0},{2,1},{3,2},{4,3},{5,4},{6,5},{7,6},{8,7},{9,8},{10,9},{11,1... | collective-permute-start | bytes 1179656 | tf_op jit(solution)/shard_map/ppermute | solution.py:784
  68.2 20.2 %collective-permute-start.8 = (f32[3,16,2048]{2,0,1:T(4,128)S(1)}, f32[3,16,2048]{2,0,1:T(4,128)S(1)}, u32[]{:S(2)}, u32[]{:S(2)}) collective-permute-start(f32[3,16,2048]{2,0,1:T(4,128)S(1)} %copy.15), channel_id=1, source_target_pairs={{0,1},{1,2},{2,3},{3,4},{4,5},{5,6},{6,7},{7,8},{8,9},{9,10},{10,1... | collective-permute-start | bytes 1179656 | tf_op jit(solution)/shard_map/ppermute | solution.py:779
  68.2 38.4 %collective-permute-start.10 = (f32[192,1024]{1,0:T(8,128)}, f32[192,1024]{1,0:T(8,128)S(1)}, u32[]{:S(2)}, u32[]{:S(2)}) collective-permute-start(f32[192,1024]{1,0:T(8,128)} %get-tuple-element.80), channel_id=1, source_target_pairs={{0,16},{16,32},{32,48},{48,64},{64,80},{80,96},{96,112},{112,0},{1... | collective-permute-start | bytes 2359304 | tf_op jit(solution)/shard_map/ppermute | solution.py:779
  68.6 40.0 %collective-permute-start.11 = (f32[192,1024]{1,0:T(8,128)}, f32[192,1024]{1,0:T(8,128)S(1)}, u32[]{:S(2)}, u32[]{:S(2)}) collective-permute-start(f32[192,1024]{1,0:T(8,128)} %get-tuple-element.81), channel_id=1, source_target_pairs={{16,0},{32,16},{48,32},{64,48},{80,64},{96,80},{112,96},{0,112},{1... | collective-permute-start | bytes 2359304 | tf_op jit(solution)/shard_map/ppermute | solution.py:784
  106.6 2.0 %copy-start.4 = (f32[192,1024]{1,0:T(8,128)}, f32[192,1024]{1,0:T(8,128)S(1)}, u32[]{:S(2)}) copy-start(f32[192,1024]{1,0:T(8,128)S(1)} %collective-permute-done.10.x_low_late) | copy-start | bytes 2359300
  108.6 0.9 copy-start.5
  144.8 10.5 %collective-permute-start.12 = (f32[9,2048]{1,0:T(8,128)}, f32[9,2048]{1,0:T(8,128)S(1)}, u32[]{:S(2)}, u32[]{:S(2)}) collective-permute-start(f32[9,2048]{1,0:T(8,128)} %get-tuple-element.98), channel_id=1, source_target_pairs={{1,0},{2,1},{3,2},{4,3},{5,4},{6,5},{7,6},{8,7},{9,8},{10,9},{11,1... | collective-permute-start | bytes 221192 | tf_op jit(solution)/shard_map/ppermute | solution.py:784
  147.7 7.6 %collective-permute-start.13 = (f32[9,2048]{1,0:T(8,128)}, f32[9,2048]{1,0:T(8,128)S(1)}, u32[]{:S(2)}, u32[]{:S(2)}) collective-permute-start(f32[9,2048]{1,0:T(8,128)} %get-tuple-element.99), channel_id=1, source_target_pairs={{0,1},{1,2},{2,3},{3,4},{4,5},{5,6},{6,7},{7,8},{8,9},{9,10},{10,1... | collective-permute-start | bytes 221192 | tf_op jit(solution)/shard_map/ppermute | solution.py:779
  155.4 10.4 %copy-start.3 = (f32[9,2048]{1,0:T(8,128)}, f32[9,2048]{1,0:T(8,128)S(1)}, u32[]{:S(2)}) copy-start(f32[9,2048]{1,0:T(8,128)S(1)} %add.11.sides_ref) | copy-start | bytes 221188
  156.3 9.5 %collective-permute-start.14 = (f32[3,2048]{1,0:T(4,128)S(1)}, f32[3,2048]{1,0:T(4,128)S(1)}, u32[]{:S(2)}, u32[]{:S(2)}) collective-permute-start(f32[3,2048]{1,0:T(4,128)S(1)} %get-tuple-element.101), channel_id=1, source_target_pairs={{16,0},{32,16},{48,32},{64,48},{80,64},{96,80},{112,96},{0,112},{1... | collective-permute-start | bytes 73736 | tf_op jit(solution)/shard_map/ppermute | solution.py:784
  158.6 7.2 %collective-permute-start.15 = (f32[3,2048]{1,0:T(4,128)S(1)}, f32[3,2048]{1,0:T(4,128)S(1)}, u32[]{:S(2)}, u32[]{:S(2)}) collective-permute-start(f32[3,2048]{1,0:T(4,128)S(1)} %get-tuple-element.102), channel_id=1, source_target_pairs={{0,16},{16,32},{32,48},{48,64},{64,80},{80,96},{96,112},{112,0},{1... | collective-permute-start | bytes 73736 | tf_op jit(solution)/shard_map/ppermute | solution.py:779
  165.8 0.6 copy-start.10
  165.8 0.6 copy-start.11

commit v3 on v2

--- a/solution.py
+++ b/solution.py
@@ -403,7 +403,7 @@
 
 X_LAYERS = 4 * HALO - 1
 X_FIRST = 2
-X_EARLY = 5
+X_EARLY = 4
 
 
 def face_rows(size_x, size_y):
@@ -812,7 +812,6 @@
     list_high = shift_down(markers_list, "gx")
     x_up_late, x_down_late = late_faces(x_up_late, x_down_late, y_low, y_high, size_x)
     mid = jnp.stack([list_low, markers_list, list_high])
-    mid, x_up_late, x_down_late = lax.optimization_barrier((mid, x_up_late, x_down_late))
     x_low_late = shift_up(x_up_late, "gx")
     x_high_late = shift_down(x_down_late, "gx")
     low = shift_up(mid, "gy")

time: 197 us -> 207 us (1.051)
  starting transfers between devices: 32.6 us -> 45.3 us
    ppermute x8, starting transfers between devices: 1.95 us -> 20.1 us  [shift_up(): return lax.ppermute(x, axis, [(i, (i + 1) % count) for i in range(count)])]
    ppermute x8, starting transfers between devices: 20.1 us -> 14.7 us  [shift_down(): return lax.ppermute(x, axis, [((i + 1) % count, i) for i in range(count)])]
  transfers between devices with their start and end apart: 17 -> 17, of which waited for: 6 -> 4; matrix products, arithmetic and copies ran while one was open for 3% -> 3% of each run, Pallas kernels for 32% -> 31%
where the time goes in v3:
time: 207 us
  Pallas kernels  104 us (50%)
  starting transfers between devices  45.3 us (22%)
  blocking collectives  23.7 us (11%)
  waiting for transfers between devices  21.7 us (10%)
  local copies, waits for them, and re-layouts  8.83 us (4%)
  other arithmetic  2.49 us (1%)
    pallas_call x1, Pallas kernels, solve(): pl.pallas_call(functools.partial(solve_kernel, sweeps), out_shape=(jax.Sh...  35.2 us
    all_to_all x1, blocking collectives, shards(): back = lax.all_to_all(back, both, split_axis=0, concat_axis=0, tiled=True)  23.7 us
    ppermute x8, starting transfers between devices, shift_up(): return lax.ppermute(x, axis, [(i, (i + 1) % count) for i in range(count)])  20.1 us
    pallas_call x1, Pallas kernels, spread_mid(): pl.pallas_call(functools.partial(spread_mid_kernel, size_x, size_y), out_...  15.6 us
    pallas_call x2, Pallas kernels, sample(): pl.pallas_call(functools.partial(sample_kernel, places), out_shape=jax.Sh...  14.9 us
    ppermute x8, starting transfers between devices, shift_down(): return lax.ppermute(x, axis, [((i + 1) % count, i) for i in range(count)])  14.7 us
    pallas_call x1, Pallas kernels, spread_side(): pl.pallas_call(functools.partial(spread_side_kernel, size_x, size_y), out...  13.9 us
    ppermute x8, waiting for transfers between devices, shift_up(): return lax.ppermute(x, axis, [(i, (i + 1) % count) for i in range(count)])  13 us
  transfers between devices with their start and end apart: 17, of which 4 were waited for; matrix products, arithmetic and copies ran while one was open for 3% of the time, Pallas kernels for 31%

profile of v3, /device:TPU:1, one launch (start us, length us, event | category | flops | bytes accessed | tf_op | source)
XLA Modules:
  0.0 206.7 jit_solution(3045501172676770029)
XLA Ops:
  0.6 1.1 slice_bitcast_fusion
  1.7 5.0 %collective-permute-start.1 = (f32[2,28,1024]{2,1,0:T(8,128)S(1)}, f32[2,28,1024]{2,1,0:T(8,128)S(1)}, u32[]{:S(2)}, u32[]{:S(2)}) collective-permute-start(f32[2,28,1024]{2,1,0:T(8,128)S(1)} %get-tuple-element.98), channel_id=1, source_target_pairs={{16,0},{32,16},{48,32},{64,48},{80,64},{96,80},{112,96},{0,112},{1... | collective-permute-start | bytes 688136 | tf_op jit(solution)/shard_map/ppermute | solution.py:784
  6.7 2.3 %pack.1 = (f32[128,256]{1,0:T(8,128)}, s32[1,1024]{1,0:T(1,128)}) custom-call(s32[1,1024]{1,0:T(1,128)} %bitcast.39, s32[3,1024]{1,0:T(4,128)} %cells_ref.1, f32[3,1024]{1,0:T(4,128)} %offsets_ref.1, f32[3,1024]{1,0:T(4,128)} %forces_ref.1), custom_call_target="tpu_custom_call" | custom-call | flops 400000000 | bytes 300000 | tf_op jit(solution)/shard_map/pack/pallas_call | solution.py:106
  9.0 1.7 copy.14
  10.6 10.5 %all-to-all-start = ((f32[128,1,256]{2,1,0:T(1,128)}), f32[128,1,256]{2,1,0:T(1,128)S(1)}, u32[]{:S(2)}, u32[]{:S(2)}) async-start(f32[128,1,256]{2,1,0:T(1,128)} %copy.14), calls=%async_computation | async-start | bytes 262144 | tf_op jit(solution)/shard_map/all_to_all | solution.py:798
  21.2 4.7 %faces.1 = (f32[56,1024]{1,0:T(8,128)}, f32[56,1024]{1,0:T(8,128)}, f32[136,1024]{1,0:T(8,128)}, f32[136,1024]{1,0:T(8,128)}, f32[200,1024]{1,0:T(8,128)}, /*index=5*/f32[200,1024]{1,0:T(8,128)}) custom-call(f32[3,12,28,1024]{3,2,1,0:T(8,128)} %vel_ref.3, f32[12,28,1024]{2,1,0:T(8,128)} %visc_ref.2), custom_call_target="tpu_custom_call" | custom-call | flops 1000000 | bytes 10000000 | tf_op jit(solution)/shard_map/faces/pallas_call | solution.py:418
  25.9 5.4 %all-to-all-done = f32[128,1,256]{2,1,0:T(1,128)S(1)} async-done(((f32[128,1,256]{2,1,0:T(1,128)}), f32[128,1,256]{2,1,0:T(1,128)S(1)}, u32[]{:S(2)}, u32[]{:S(2)}) %all-to-all-start) | async-done | bytes 131104 | tf_op jit(solution)/shard_map/all_to_all | solution.py:798
  31.3 0.7 copy.28
  32.0 0.0 collective-permute-done.1.x_high_first
  32.0 0.0 collective-permute-done.x_low_first
  32.0 0.7 copy-done.7
  32.7 0.6 collective-permute-start.4
  33.3 0.0 collective-permute-start.5
  33.3 0.6 collective-permute-start.2
  33.9 3.0 %collective-permute-start.3 = (f32[56,1024]{1,0:T(8,128)}, f32[56,1024]{1,0:T(8,128)S(1)}, u32[]{:S(2)}, u32[]{:S(2)}) collective-permute-start(f32[56,1024]{1,0:T(8,128)} %get-tuple-element.60), channel_id=1, source_target_pairs={{16,0},{32,16},{48,32},{64,48},{80,64},{96,80},{112,96},{0,112},{1... | collective-permute-start | bytes 688136 | tf_op jit(solution)/shard_map/ppermute | solution.py:784
  36.9 9.3 %sort.1 = (f32[16,2048]{1,0:T(8,128)}, s32[16,128]{1,0:T(8,128)}) custom-call(f32[128,256]{1,0:T(8,128)} %bitcast.32), custom_call_target="tpu_custom_call" | custom-call | flops 2000000000 | bytes 300000 | tf_op jit(solution)/shard_map/sort/pallas_call | solution.py:200
  46.2 2.2 %collective-permute-done.2.x_low = f32[56,1024]{1,0:T(8,128)S(1)} collective-permute-done((f32[56,1024]{1,0:T(8,128)}, f32[56,1024]{1,0:T(8,128)S(1)}, u32[]{:S(2)}, u32[]{:S(2)}) %collective-permute-start.2) | collective-permute-done | bytes 229408 | tf_op jit(solution)/shard_map/ppermute | solution.py:779
  48.5 3.2 %collective-permute-done.3.x_high = f32[56,1024]{1,0:T(8,128)S(1)} collective-permute-done((f32[56,1024]{1,0:T(8,128)}, f32[56,1024]{1,0:T(8,128)S(1)}, u32[]{:S(2)}, u32[]{:S(2)}) %collective-permute-start.3) | collective-permute-done | bytes 229408 | tf_op jit(solution)/shard_map/ppermute | solution.py:784
  51.7 1.1 collective-permute-start.7
  52.8 0.4 collective-permute-start.6
  53.3 3.1 %late_faces.1 = (f32[224,1024]{1,0:T(8,128)}, f32[224,1024]{1,0:T(8,128)}) custom-call(f32[200,1024]{1,0:T(8,128)} %get-tuple-element.70.up_ref, f32[200,1024]{1,0:T(8,128)} %get-tuple-element.71.down_ref, f32[136,1024]{1,0:T(8,128)} %copy-done.1, f32[136,1024]{1,0:T(8,128)} %copy-done.2), custom_call_target="tpu_custom_call" | custom-call | flops 1000000 | bytes 4000000 | tf_op jit(solution)/shard_map/late_faces/pallas_call | solution.py:462
  56.4 0.5 collective-permute-start.10
  56.9 3.0 %collective-permute-start.11 = (f32[224,1024]{1,0:T(8,128)}, f32[224,1024]{1,0:T(8,128)S(1)}, u32[]{:S(2)}, u32[]{:S(2)}) collective-permute-start(f32[224,1024]{1,0:T(8,128)} %get-tuple-element.75), channel_id=1, source_target_pairs={{16,0},{32,16},{48,32},{64,48},{80,64},{96,80},{112,96},{0,112},{1... | collective-permute-start | bytes 2752520 | tf_op jit(solution)/shard_map/ppermute | solution.py:784
  60.0 0.0 collective-permute-done.7
  60.0 0.9 pad_maximum_fusion.mid_ref
  60.9 0.3 copy.15
  61.2 2.5 %collective-permute-start.9 = (f32[3,16,2048]{2,0,1:T(4,128)S(1)}, f32[3,16,2048]{2,0,1:T(4,128)S(1)}, u32[]{:S(2)}, u32[]{:S(2)}) collective-permute-start(f32[3,16,2048]{2,0,1:T(4,128)S(1)} %copy.15), channel_id=1, source_target_pairs={{1,0},{2,1},{3,2},{4,3},{5,4},{6,5},{7,6},{8,7},{9,8},{10,9},{11,1... | collective-permute-start | bytes 1179656 | tf_op jit(solution)/shard_map/ppermute | solution.py:784
  63.7 14.8 %collective-permute-start.8 = (f32[3,16,2048]{2,0,1:T(4,128)S(1)}, f32[3,16,2048]{2,0,1:T(4,128)S(1)}, u32[]{:S(2)}, u32[]{:S(2)}) collective-permute-start(f32[3,16,2048]{2,0,1:T(4,128)S(1)} %copy.15), channel_id=1, source_target_pairs={{0,1},{1,2},{2,3},{3,4},{4,5},{5,6},{6,7},{7,8},{8,9},{9,10},{10,1... | collective-permute-start | bytes 1179656 | tf_op jit(solution)/shard_map/ppermute | solution.py:779
  78.5 0.6 pad.4.meta
  79.1 15.6 %spread_mid.1.spread_ref = f32[3,18,40,1024]{3,2,1,0:T(8,128)} custom-call(s32[9,64]{1,0:T(8,128)} %pad.4.meta, f32[3,16,2048]{2,1,0:T(8,128)} %copy-done), custom_call_target="tpu_custom_call" | custom-call | flops 10000000000 | bytes 10000000 | tf_op jit(solution)/shard_map/spread_mid/pallas_call | solution.py:350
  94.7 1.0 copy.17.low_ref
  95.7 1.0 copy.18.high_ref
  96.6 0.6 maximum_convert_fusion.meta
  97.2 13.9 %spread_side.1 = (f32[3,18,8,1024]{3,2,1,0:T(8,128)}, f32[3,18,8,1024]{3,2,1,0:T(8,128)}) custom-call(s32[9,64]{1,0:T(8,128)} %maximum_convert_fusion.meta, f32[3,16,2048]{2,1,0:T(8,128)} %copy.17.low_ref, f32[3,16,2048]{2,1,0:T(8,128)} %copy.18.high_ref), custom_call_target="tpu_custom_call" | custom-call | flops 10000000000 | bytes 10000000 | tf_op jit(solution)/shard_map/spread_side/pallas_call | solution.py:363
  111.1 1.0 copy-done.4
  112.1 0.3 copy-done.5
  112.4 35.2 %solve.1 = (f32[3,12,28,1024]{3,2,1,0:T(8,128)}, f32[9,2048]{1,0:T(8,128)}, f32[9,2048]{1,0:T(8,128)}) custom-call(s32[9,64]{1,0:T(8,128)} %maximum_convert_fusion.meta, f32[3,18,40,1024]{3,2,1,0:T(8,128)} %spread_mid.1.spread_ref, f32[3,18,8,1024]{3,2,1,0:T(8,128)} %get-tuple-element.80.side_low, f32[3,18,8,1024]{3,2,1,0:T(8,128)} %get-tuple-element.81.side_high, ...), custom_call_target="tpu_custom_call" | custom-call | flops 10000000000 | bytes 20000000 | tf_op jit(solution)/shard_map/solve/pallas_call | solution.py:698
  147.5 1.7 collective-permute-start.13
  149.3 7.7 %sample.2 = f32[2,8,2048]{2,1,0:T(8,128)} custom-call(s32[9,64]{1,0:T(8,128)} %maximum_convert_fusion.meta, f32[3,16,2048]{2,1,0:T(8,128)} %copy-done, f32[3,12,28,1024]{3,2,1,0:T(8,128)} %get-tuple-element.94.field), custom_call_target="tpu_custom_call" | custom-call | flops 5000000000 | bytes 5000000 | tf_op jit(solution)/shard_map/sample/pallas_call | solution.py:682
  157.0 0.9 fusion
  157.9 0.1 collective-permute-start.14
  158.0 1.5 collective-permute-start.15
  159.5 7.2 %sample.3.own_ref = f32[1,8,2048]{2,1,0:T(8,128)} custom-call(s32[9,64]{1,0:T(8,128)} %maximum_convert_fusion.meta, f32[3,16,2048]{2,1,0:T(8,128)} %copy-done, f32[3,12,28,1024]{3,2,1,0:T(8,128)} %get-tuple-element.94.field), custom_call_target="tpu_custom_call" | custom-call | flops 5000000000 | bytes 5000000 | tf_op jit(solution)/shard_map/sample/pallas_call | solution.py:682
  166.7 10.7 %collective-permute-done.15.high_ref = f32[3,2048]{1,0:T(4,128)S(1)} collective-permute-done((f32[3,2048]{1,0:T(4,128)S(1)}, f32[3,2048]{1,0:T(4,128)S(1)}, u32[]{:S(2)}, u32[]{:S(2)}) %collective-permute-start.15) | collective-permute-done | bytes 24608 | tf_op jit(solution)/shard_map/ppermute | solution.py:779
  177.4 0.6 copy-done.11
  178.0 3.2 %unsort.1 = f32[128,128]{1,0:T(8,128)} custom-call(f32[1,8,2048]{2,1,0:T(8,128)} %sample.3.own_ref, f32[9,2048]{1,0:T(8,128)} %copy-done.3, f32[3,2048]{1,0:T(4,128)} %copy-done.10, f32[3,2048]{1,0:T(4,128)} %copy-done.11, s32[16,128]{1,0:T(8,128)} %get-tuple-element.97.rank_ref), custom_call_target="tpu_custom_call" | custom-call | flops 1000000000 | bytes 300000 | tf_op jit(solution)/shard_map/unsort/pallas_call | solution.py:737
  181.1 23.7 %all_to_all.23 = f32[128,1,128]{2,1,0:T(1,128)} all-to-all(f32[128,1,128]{2,1,0:T(1,128)} %bitcast.37), channel_id=1, replica_groups=mesh['gx'=8,'gy'=16] {'gx','gy'}, dimensions={0} | all-to-all | bytes 131072 | tf_op jit(solution)/shard_map/all_to_all | solution.py:837
  204.8 1.9 unpack.1
  (36 shorter events, 0.1 us)
Async XLA Ops:
  1.7 30.3 %collective-permute-start.1 = (f32[2,28,1024]{2,1,0:T(8,128)S(1)}, f32[2,28,1024]{2,1,0:T(8,128)S(1)}, u32[]{:S(2)}, u32[]{:S(2)}) collective-permute-start(f32[2,28,1024]{2,1,0:T(8,128)S(1)} %get-tuple-element.98), channel_id=1, source_target_pairs={{16,0},{32,16},{48,32},{64,48},{80,64},{96,80},{112,96},{0,112},{1... | collective-permute-start | bytes 688136 | tf_op jit(solution)/shard_map/ppermute | solution.py:784
  6.7 25.3 %collective-permute-start = (f32[2,28,1024]{2,1,0:T(8,128)S(1)}, f32[2,28,1024]{2,1,0:T(8,128)S(1)}, u32[]{:S(2)}, u32[]{:S(2)}) collective-permute-start(f32[2,28,1024]{2,1,0:T(8,128)S(1)} %get-tuple-element.99), channel_id=1, source_target_pairs={{0,16},{16,32},{32,48},{48,64},{64,80},{80,96},{96,112},{112,0},{1... | collective-permute-start | bytes 688136 | tf_op jit(solution)/shard_map/ppermute | solution.py:779
  10.6 20.7 %all-to-all-start = ((f32[128,1,256]{2,1,0:T(1,128)}), f32[128,1,256]{2,1,0:T(1,128)S(1)}, u32[]{:S(2)}, u32[]{:S(2)}) async-start(f32[128,1,256]{2,1,0:T(1,128)} %copy.14), calls=%async_computation | async-start | bytes 262144 | tf_op jit(solution)/shard_map/all_to_all | solution.py:798
  32.0 24.4 %copy-start.6 = (f32[2,28,1024]{2,1,0:T(8,128)}, f32[2,28,1024]{2,1,0:T(8,128)S(1)}, u32[]{:S(2)}) copy-start(f32[2,28,1024]{2,1,0:T(8,128)S(1)} %collective-permute-done.1.x_high_first) | copy-start | bytes 688132
  32.0 0.7 copy-start.7
  32.7 19.0 %collective-permute-start.4 = (f32[136,1024]{1,0:T(8,128)}, f32[136,1024]{1,0:T(8,128)S(1)}, u32[]{:S(2)}, u32[]{:S(2)}) collective-permute-start(f32[136,1024]{1,0:T(8,128)} %get-tuple-element.61), channel_id=1, source_target_pairs={{0,1},{1,2},{2,3},{3,4},{4,5},{5,6},{6,7},{7,8},{8,9},{9,10},{10,1... | collective-permute-start | bytes 1671176 | tf_op jit(solution)/shard_map/ppermute | solution.py:779
  33.3 18.4 %collective-permute-start.5 = (f32[136,1024]{1,0:T(8,128)}, f32[136,1024]{1,0:T(8,128)S(1)}, u32[]{:S(2)}, u32[]{:S(2)}) collective-permute-start(f32[136,1024]{1,0:T(8,128)} %get-tuple-element.62), channel_id=1, source_target_pairs={{1,0},{2,1},{3,2},{4,3},{5,4},{6,5},{7,6},{8,7},{9,8},{10,9},{11,1... | collective-permute-start | bytes 1671176 | tf_op jit(solution)/shard_map/ppermute | solution.py:784
  33.3 15.1 %collective-permute-start.2 = (f32[56,1024]{1,0:T(8,128)}, f32[56,1024]{1,0:T(8,128)S(1)}, u32[]{:S(2)}, u32[]{:S(2)}) collective-permute-start(f32[56,1024]{1,0:T(8,128)} %get-tuple-element.59), channel_id=1, source_target_pairs={{0,16},{16,32},{32,48},{48,64},{64,80},{80,96},{96,112},{112,0},{1... | collective-permute-start | bytes 688136 | tf_op jit(solution)/shard_map/ppermute | solution.py:779
  33.9 17.8 %collective-permute-start.3 = (f32[56,1024]{1,0:T(8,128)}, f32[56,1024]{1,0:T(8,128)S(1)}, u32[]{:S(2)}, u32[]{:S(2)}) collective-permute-start(f32[56,1024]{1,0:T(8,128)} %get-tuple-element.60), channel_id=1, source_target_pairs={{16,0},{32,16},{48,32},{64,48},{80,64},{96,80},{112,96},{0,112},{1... | collective-permute-start | bytes 688136 | tf_op jit(solution)/shard_map/ppermute | solution.py:784
  48.5 8.5 %copy-start.8 = (f32[56,1024]{1,0:T(8,128)}, f32[56,1024]{1,0:T(8,128)S(1)}, u32[]{:S(2)}) copy-start(f32[56,1024]{1,0:T(8,128)S(1)} %collective-permute-done.2.x_low) | copy-start | bytes 688132
  51.7 5.2 %copy-start.9 = (f32[56,1024]{1,0:T(8,128)}, f32[56,1024]{1,0:T(8,128)S(1)}, u32[]{:S(2)}) copy-start(f32[56,1024]{1,0:T(8,128)S(1)} %collective-permute-done.3.x_high) | copy-start | bytes 688132
  51.7 1.6 copy-start.1
  51.7 1.6 copy-start.2
  51.7 8.2 %collective-permute-start.7 = (f32[16,2048]{1,0:T(8,128)}, f32[16,2048]{1,0:T(8,128)S(1)}, u32[]{:S(2)}, u32[]{:S(2)}) collective-permute-start(f32[16,2048]{1,0:T(8,128)} %get-tuple-element.63), channel_id=1, source_target_pairs={{16,0},{32,16},{48,32},{64,48},{80,64},{96,80},{112,96},{0,112},{1... | collective-permute-start | bytes 393224 | tf_op jit(solution)/shard_map/ppermute | solution.py:784
  52.8 7.1 %collective-permute-start.6 = (f32[16,2048]{1,0:T(8,128)}, f32[16,2048]{1,0:T(8,128)S(1)}, u32[]{:S(2)}, u32[]{:S(2)}) collective-permute-start(f32[16,2048]{1,0:T(8,128)} %get-tuple-element.63), channel_id=1, source_target_pairs={{0,16},{16,32},{32,48},{48,64},{64,80},{80,96},{96,112},{112,0},{1... | collective-permute-start | bytes 393224 | tf_op jit(solution)/shard_map/ppermute | solution.py:779
  56.4 54.7 %collective-permute-start.10 = (f32[224,1024]{1,0:T(8,128)}, f32[224,1024]{1,0:T(8,128)S(1)}, u32[]{:S(2)}, u32[]{:S(2)}) collective-permute-start(f32[224,1024]{1,0:T(8,128)} %get-tuple-element.74), channel_id=1, source_target_pairs={{0,16},{16,32},{32,48},{48,64},{64,80},{80,96},{96,112},{112,0},{1... | collective-permute-start | bytes 2752520 | tf_op jit(solution)/shard_map/ppermute | solution.py:779
  56.9 54.2 %collective-permute-start.11 = (f32[224,1024]{1,0:T(8,128)}, f32[224,1024]{1,0:T(8,128)S(1)}, u32[]{:S(2)}, u32[]{:S(2)}) collective-permute-start(f32[224,1024]{1,0:T(8,128)} %get-tuple-element.75), channel_id=1, source_target_pairs={{16,0},{32,16},{48,32},{64,48},{80,64},{96,80},{112,96},{0,112},{1... | collective-permute-start | bytes 2752520 | tf_op jit(solution)/shard_map/ppermute | solution.py:784
  60.9 18.2 %copy-start = (f32[3,16,2048]{2,1,0:T(8,128)}, f32[3,16,2048]{2,1,0:T(8,128)S(1)}, u32[]{:S(2)}) copy-start(f32[3,16,2048]{2,1,0:T(8,128)S(1)} %pad_maximum_fusion.mid_ref) | copy-start | bytes 1179652
  61.2 33.5 %collective-permute-start.9 = (f32[3,16,2048]{2,0,1:T(4,128)S(1)}, f32[3,16,2048]{2,0,1:T(4,128)S(1)}, u32[]{:S(2)}, u32[]{:S(2)}) collective-permute-start(f32[3,16,2048]{2,0,1:T(4,128)S(1)} %copy.15), channel_id=1, source_target_pairs={{1,0},{2,1},{3,2},{4,3},{5,4},{6,5},{7,6},{8,7},{9,8},{10,9},{11,1... | collective-permute-start | bytes 1179656 | tf_op jit(solution)/shard_map/ppermute | solution.py:784
  63.7 31.0 %collective-permute-start.8 = (f32[3,16,2048]{2,0,1:T(4,128)S(1)}, f32[3,16,2048]{2,0,1:T(4,128)S(1)}, u32[]{:S(2)}, u32[]{:S(2)}) collective-permute-start(f32[3,16,2048]{2,0,1:T(4,128)S(1)} %copy.15), channel_id=1, source_target_pairs={{0,1},{1,2},{2,3},{3,4},{4,5},{5,6},{6,7},{7,8},{8,9},{9,10},{10,1... | collective-permute-start | bytes 1179656 | tf_op jit(solution)/shard_map/ppermute | solution.py:779
  111.1 1.0 copy-start.4
  111.1 1.2 copy-start.5
  147.5 9.4 %collective-permute-start.12 = (f32[9,2048]{1,0:T(8,128)}, f32[9,2048]{1,0:T(8,128)S(1)}, u32[]{:S(2)}, u32[]{:S(2)}) collective-permute-start(f32[9,2048]{1,0:T(8,128)} %get-tuple-element.92), channel_id=1, source_target_pairs={{1,0},{2,1},{3,2},{4,3},{5,4},{6,5},{7,6},{8,7},{9,8},{10,9},{11,1... | collective-permute-start | bytes 221192 | tf_op jit(solution)/shard_map/ppermute | solution.py:784
  147.5 9.4 %collective-permute-start.13 = (f32[9,2048]{1,0:T(8,128)}, f32[9,2048]{1,0:T(8,128)S(1)}, u32[]{:S(2)}, u32[]{:S(2)}) collective-permute-start(f32[9,2048]{1,0:T(8,128)} %get-tuple-element.93), channel_id=1, source_target_pairs={{0,1},{1,2},{2,3},{3,4},{4,5},{5,6},{6,7},{7,8},{8,9},{9,10},{10,1... | collective-permute-start | bytes 221192 | tf_op jit(solution)/shard_map/ppermute | solution.py:779
  157.0 9.7 %copy-start.3 = (f32[9,2048]{1,0:T(8,128)}, f32[9,2048]{1,0:T(8,128)S(1)}, u32[]{:S(2)}) copy-start(f32[9,2048]{1,0:T(8,128)S(1)} %add.11.sides_ref) | copy-start | bytes 221188
  157.9 8.7 %collective-permute-start.14 = (f32[3,2048]{1,0:T(4,128)S(1)}, f32[3,2048]{1,0:T(4,128)S(1)}, u32[]{:S(2)}, u32[]{:S(2)}) collective-permute-start(f32[3,2048]{1,0:T(4,128)S(1)} %get-tuple-element.95), channel_id=1, source_target_pairs={{16,0},{32,16},{48,32},{64,48},{80,64},{96,80},{112,96},{0,112},{1... | collective-permute-start | bytes 73736 | tf_op jit(solution)/shard_map/ppermute | solution.py:784
  158.0 19.4 %collective-permute-start.15 = (f32[3,2048]{1,0:T(4,128)S(1)}, f32[3,2048]{1,0:T(4,128)S(1)}, u32[]{:S(2)}, u32[]{:S(2)}) collective-permute-start(f32[3,2048]{1,0:T(4,128)S(1)} %get-tuple-element.96), channel_id=1, source_target_pairs={{0,16},{16,32},{32,48},{48,64},{64,80},{80,96},{96,112},{112,0},{1... | collective-permute-start | bytes 73736 | tf_op jit(solution)/shard_map/ppermute | solution.py:779
  166.6 10.7 %copy-start.10 = (f32[3,2048]{1,0:T(4,128)}, f32[3,2048]{1,0:T(4,128)S(1)}, u32[]{:S(2)}) copy-start(f32[3,2048]{1,0:T(4,128)S(1)} %collective-permute-done.14.low_ref) | copy-start | bytes 73732
  177.4 0.6 copy-start.11

commit v4 on v2

--- a/solution.py
+++ b/solution.py
@@ -402,7 +402,7 @@
 
 
 X_LAYERS = 4 * HALO - 1
-X_FIRST = 2
+X_FIRST = 3
 X_EARLY = 5
 
 

time: 197 us -> 195 us (0.990)
  waiting for transfers between devices: 22.8 us -> 17.1 us
    ppermute x8, waiting for transfers between devices: 12.1 us -> 6.38 us  [shift_up(): return lax.ppermute(x, axis, [(i, (i + 1) % count) for i in range(count)])]
  transfers between devices with their start and end apart: 17 -> 17, of which waited for: 6 -> 7; matrix products, arithmetic and copies ran while one was open for 3% -> 3% of each run, Pallas kernels for 32% -> 32%
where the time goes in v4:
time: 195 us; the launch traced here: 196 us
  Pallas kernels  104 us (53%)
  starting transfers between devices  33.9 us (17%)
  blocking collectives  27.6 us (14%)
  waiting for transfers between devices  17.1 us (9%)
  local copies, waits for them, and re-layouts  9.34 us (5%)
  other arithmetic  2.49 us (1%)
    pallas_call x1, Pallas kernels, solve(): pl.pallas_call(functools.partial(solve_kernel, sweeps), out_shape=(jax.Sh...  36.4 us
    all_to_all x1, blocking collectives, shards(): back = lax.all_to_all(back, both, split_axis=0, concat_axis=0, tiled=True)  27.6 us
    ppermute x8, starting transfers between devices, shift_down(): return lax.ppermute(x, axis, [((i + 1) % count, i) for i in range(count)])  21.3 us
    pallas_call x1, Pallas kernels, spread_side(): pl.pallas_call(functools.partial(spread_side_kernel, size_x, size_y), out...  15.4 us
    pallas_call x1, Pallas kernels, spread_mid(): pl.pallas_call(functools.partial(spread_mid_kernel, size_x, size_y), out_...  14.5 us
    pallas_call x2, Pallas kernels, sample(): pl.pallas_call(functools.partial(sample_kernel, places), out_shape=jax.Sh...  13.9 us
    all_to_all x1, starting transfers between devices, shards(): lax.all_to_all(outgoing, both, split_axis=0, concat_axis=0, tiled=True)  10.5 us
    pallas_call x1, Pallas kernels, sort(): pl.pallas_call(functools.partial(sort_kernel, depth), out_shape=(jax.Shap...  9.33 us
  transfers between devices with their start and end apart: 17, of which 7 were waited for; matrix products, arithmetic and copies ran while one was open for 3% of the time, Pallas kernels for 32%

profile of v4, /device:TPU:1, one launch (start us, length us, event | category | flops | bytes accessed | tf_op | source)
XLA Modules:
  0.0 195.5 jit_solution(5436640996915831638)
XLA Ops:
  0.6 1.2 slice_bitcast_fusion
  1.8 5.0 %collective-permute-start.1 = (f32[3,28,1024]{2,1,0:T(8,128)S(1)}, f32[3,28,1024]{2,1,0:T(8,128)S(1)}, u32[]{:S(2)}, u32[]{:S(2)}) collective-permute-start(f32[3,28,1024]{2,1,0:T(8,128)S(1)} %get-tuple-element.104), channel_id=1, source_target_pairs={{16,0},{32,16},{48,32},{64,48},{80,64},{96,80},{112,96},{0,112},{1... | collective-permute-start | bytes 1032200 | tf_op jit(solution)/shard_map/ppermute | solution.py:784
  6.8 0.0 collective-permute-start
  6.8 2.3 %pack.1 = (f32[128,256]{1,0:T(8,128)}, s32[1,1024]{1,0:T(1,128)}) custom-call(s32[1,1024]{1,0:T(1,128)} %bitcast.39, s32[3,1024]{1,0:T(4,128)} %cells_ref.1, f32[3,1024]{1,0:T(4,128)} %offsets_ref.1, f32[3,1024]{1,0:T(4,128)} %forces_ref.1), custom_call_target="tpu_custom_call" | custom-call | flops 400000000 | bytes 300000 | tf_op jit(solution)/shard_map/pack/pallas_call | solution.py:106
  9.0 1.7 copy.14
  10.7 10.5 %all-to-all-start = ((f32[128,1,256]{2,1,0:T(1,128)}), f32[128,1,256]{2,1,0:T(1,128)S(1)}, u32[]{:S(2)}, u32[]{:S(2)}) async-start(f32[128,1,256]{2,1,0:T(1,128)} %copy.14), calls=%async_computation | async-start | bytes 262144 | tf_op jit(solution)/shard_map/all_to_all | solution.py:798
  21.3 4.7 %faces.1 = (f32[56,1024]{1,0:T(8,128)}, f32[56,1024]{1,0:T(8,128)}, f32[136,1024]{1,0:T(8,128)}, f32[136,1024]{1,0:T(8,128)}, f32[168,1024]{1,0:T(8,128)}, /*index=5*/f32[168,1024]{1,0:T(8,128)}) custom-call(f32[3,12,28,1024]{3,2,1,0:T(8,128)} %vel_ref.3, f32[12,28,1024]{2,1,0:T(8,128)} %visc_ref.2), custom_call_target="tpu_custom_call" | custom-call | flops 1000000 | bytes 10000000 | tf_op jit(solution)/shard_map/faces/pallas_call | solution.py:418
  25.9 5.5 %all-to-all-done = f32[128,1,256]{2,1,0:T(1,128)S(1)} async-done(((f32[128,1,256]{2,1,0:T(1,128)}), f32[128,1,256]{2,1,0:T(1,128)S(1)}, u32[]{:S(2)}, u32[]{:S(2)}) %all-to-all-start) | async-done | bytes 131104 | tf_op jit(solution)/shard_map/all_to_all | solution.py:798
  31.4 0.7 copy.28
  32.1 0.8 copy-done.7
  32.9 0.6 collective-permute-start.4
  33.5 0.6 collective-permute-start.2
  34.0 3.0 %collective-permute-start.3 = (f32[56,1024]{1,0:T(8,128)}, f32[56,1024]{1,0:T(8,128)S(1)}, u32[]{:S(2)}, u32[]{:S(2)}) collective-permute-start(f32[56,1024]{1,0:T(8,128)} %get-tuple-element.63), channel_id=1, source_target_pairs={{16,0},{32,16},{48,32},{64,48},{80,64},{96,80},{112,96},{0,112},{1... | collective-permute-start | bytes 688136 | tf_op jit(solution)/shard_map/ppermute | solution.py:784
  37.1 9.3 %sort.1 = (f32[16,2048]{1,0:T(8,128)}, s32[16,128]{1,0:T(8,128)}) custom-call(f32[128,256]{1,0:T(8,128)} %bitcast.32), custom_call_target="tpu_custom_call" | custom-call | flops 2000000000 | bytes 300000 | tf_op jit(solution)/shard_map/sort/pallas_call | solution.py:200
  46.4 2.2 %collective-permute-done.2.x_low = f32[56,1024]{1,0:T(8,128)S(1)} collective-permute-done((f32[56,1024]{1,0:T(8,128)}, f32[56,1024]{1,0:T(8,128)S(1)}, u32[]{:S(2)}, u32[]{:S(2)}) %collective-permute-start.2) | collective-permute-done | bytes 229408 | tf_op jit(solution)/shard_map/ppermute | solution.py:779
  48.6 3.2 %collective-permute-done.3.x_high = f32[56,1024]{1,0:T(8,128)S(1)} collective-permute-done((f32[56,1024]{1,0:T(8,128)}, f32[56,1024]{1,0:T(8,128)S(1)}, u32[]{:S(2)}, u32[]{:S(2)}) %collective-permute-start.3) | collective-permute-done | bytes 229408 | tf_op jit(solution)/shard_map/ppermute | solution.py:784
  51.9 0.7 copy-done.9
  52.5 1.0 collective-permute-start.7
  53.6 0.4 collective-permute-start.6
  54.0 2.9 %late_faces.1 = (f32[192,1024]{1,0:T(8,128)}, f32[192,1024]{1,0:T(8,128)}) custom-call(f32[168,1024]{1,0:T(8,128)} %get-tuple-element.67.up_ref, f32[168,1024]{1,0:T(8,128)} %get-tuple-element.68.down_ref, f32[136,1024]{1,0:T(8,128)} %copy-done.1, f32[136,1024]{1,0:T(8,128)} %copy-done.2), custom_call_target="tpu_custom_call" | custom-call | flops 1000000 | bytes 4000000 | tf_op jit(solution)/shard_map/late_faces/pallas_call | solution.py:462
  57.0 2.8 %collective-permute-done.6 = f32[16,2048]{1,0:T(8,128)S(1)} collective-permute-done((f32[16,2048]{1,0:T(8,128)}, f32[16,2048]{1,0:T(8,128)S(1)}, u32[]{:S(2)}, u32[]{:S(2)}) %collective-permute-start.6) | collective-permute-done | bytes 131104 | tf_op jit(solution)/shard_map/ppermute | solution.py:779
  59.7 0.9 pad_maximum_fusion.mid_ref
  60.7 0.3 copy.15
  61.0 2.3 %collective-permute-start.9 = (f32[3,16,2048]{2,0,1:T(4,128)S(1)}, f32[3,16,2048]{2,0,1:T(4,128)S(1)}, u32[]{:S(2)}, u32[]{:S(2)}) collective-permute-start(f32[3,16,2048]{2,0,1:T(4,128)S(1)} %copy.15), channel_id=1, source_target_pairs={{1,0},{2,1},{3,2},{4,3},{5,4},{6,5},{7,6},{8,7},{9,8},{10,9},{11,1... | collective-permute-start | bytes 1179656 | tf_op jit(solution)/shard_map/ppermute | solution.py:784
  63.3 0.3 collective-permute-start.10
  63.5 3.6 %collective-permute-start.11 = (f32[192,1024]{1,0:T(8,128)}, f32[192,1024]{1,0:T(8,128)S(1)}, u32[]{:S(2)}, u32[]{:S(2)}) collective-permute-start(f32[192,1024]{1,0:T(8,128)} %get-tuple-element.81), channel_id=1, source_target_pairs={{16,0},{32,16},{48,32},{64,48},{80,64},{96,80},{112,96},{0,112},{1... | collective-permute-start | bytes 2359304 | tf_op jit(solution)/shard_map/ppermute | solution.py:784
  67.2 0.6 pad.4.meta
  67.8 14.5 %spread_mid.1.spread_ref = f32[3,18,40,1024]{3,2,1,0:T(8,128)} custom-call(s32[9,64]{1,0:T(8,128)} %pad.4.meta, f32[3,16,2048]{2,1,0:T(8,128)} %copy-done), custom_call_target="tpu_custom_call" | custom-call | flops 10000000000 | bytes 10000000 | tf_op jit(solution)/shard_map/spread_mid/pallas_call | solution.py:350
  82.2 1.0 copy.17.low_ref
  83.2 1.0 copy.18.high_ref
  84.2 0.6 maximum_convert_fusion.meta
  84.8 15.4 %spread_side.1 = (f32[3,18,8,1024]{3,2,1,0:T(8,128)}, f32[3,18,8,1024]{3,2,1,0:T(8,128)}) custom-call(s32[9,64]{1,0:T(8,128)} %maximum_convert_fusion.meta, f32[3,16,2048]{2,1,0:T(8,128)} %copy.17.low_ref, f32[3,16,2048]{2,1,0:T(8,128)} %copy.18.high_ref), custom_call_target="tpu_custom_call" | custom-call | flops 10000000000 | bytes 10000000 | tf_op jit(solution)/shard_map/spread_side/pallas_call | solution.py:363
  100.2 1.3 collective-permute-done.10.x_low_late
  101.5 2.0 %collective-permute-done.11.x_high_late = f32[192,1024]{1,0:T(8,128)S(1)} collective-permute-done((f32[192,1024]{1,0:T(8,128)}, f32[192,1024]{1,0:T(8,128)S(1)}, u32[]{:S(2)}, u32[]{:S(2)}) %collective-permute-start.11) | collective-permute-done | bytes 786464 | tf_op jit(solution)/shard_map/ppermute | solution.py:784
  103.5 0.9 copy-done.5
  104.4 36.4 %solve.1 = (f32[3,12,28,1024]{3,2,1,0:T(8,128)}, f32[9,2048]{1,0:T(8,128)}, f32[9,2048]{1,0:T(8,128)}) custom-call(s32[9,64]{1,0:T(8,128)} %maximum_convert_fusion.meta, f32[3,18,40,1024]{3,2,1,0:T(8,128)} %spread_mid.1.spread_ref, f32[3,18,8,1024]{3,2,1,0:T(8,128)} %get-tuple-element.86.side_low, f32[3,18,8,1024]{3,2,1,0:T(8,128)} %get-tuple-element.87.side_high, ...), custom_call_target="tpu_custom_call" | custom-call | flops 10000000000 | bytes 20000000 | tf_op jit(solution)/shard_map/solve/pallas_call | solution.py:698
  140.8 1.5 collective-permute-start.12
  142.2 0.3 collective-permute-start.13
  142.5 6.7 %sample.2 = f32[2,8,2048]{2,1,0:T(8,128)} custom-call(s32[9,64]{1,0:T(8,128)} %maximum_convert_fusion.meta, f32[3,16,2048]{2,1,0:T(8,128)} %copy-done, f32[3,12,28,1024]{3,2,1,0:T(8,128)} %get-tuple-element.100.field), custom_call_target="tpu_custom_call" | custom-call | flops 5000000000 | bytes 5000000 | tf_op jit(solution)/shard_map/sample/pallas_call | solution.py:682
  149.2 0.1 collective-permute-done.13
  149.3 0.9 fusion
  150.3 4.8 %collective-permute-start.14 = (f32[3,2048]{1,0:T(4,128)S(1)}, f32[3,2048]{1,0:T(4,128)S(1)}, u32[]{:S(2)}, u32[]{:S(2)}) collective-permute-start(f32[3,2048]{1,0:T(4,128)S(1)} %get-tuple-element.101), channel_id=1, source_target_pairs={{16,0},{32,16},{48,32},{64,48},{80,64},{96,80},{112,96},{0,112},{1... | collective-permute-start | bytes 73736 | tf_op jit(solution)/shard_map/ppermute | solution.py:784
  155.1 7.2 %sample.3.own_ref = f32[1,8,2048]{2,1,0:T(8,128)} custom-call(s32[9,64]{1,0:T(8,128)} %maximum_convert_fusion.meta, f32[3,16,2048]{2,1,0:T(8,128)} %copy-done, f32[3,12,28,1024]{3,2,1,0:T(8,128)} %get-tuple-element.100.field), custom_call_target="tpu_custom_call" | custom-call | flops 5000000000 | bytes 5000000 | tf_op jit(solution)/shard_map/sample/pallas_call | solution.py:682
  162.3 0.6 copy-done.10
  162.9 0.0 copy-done.11
  162.9 3.2 %unsort.1 = f32[128,128]{1,0:T(8,128)} custom-call(f32[1,8,2048]{2,1,0:T(8,128)} %sample.3.own_ref, f32[9,2048]{1,0:T(8,128)} %copy-done.3, f32[3,2048]{1,0:T(4,128)} %copy-done.10, f32[3,2048]{1,0:T(4,128)} %copy-done.11, s32[16,128]{1,0:T(8,128)} %get-tuple-element.103.rank_ref), custom_call_target="tpu_custom_call" | custom-call | flops 1000000000 | bytes 300000 | tf_op jit(solution)/shard_map/unsort/pallas_call | solution.py:737
  166.1 27.6 %all_to_all.23 = f32[128,1,128]{2,1,0:T(1,128)} all-to-all(f32[128,1,128]{2,1,0:T(1,128)} %bitcast.37), channel_id=1, replica_groups=mesh['gx'=8,'gy'=16] {'gx','gy'}, dimensions={0} | all-to-all | bytes 131072 | tf_op jit(solution)/shard_map/all_to_all | solution.py:838
  193.6 1.9 unpack.1
  (36 shorter events, 0.1 us)
Async XLA Ops:
  1.8 30.3 %collective-permute-start.1 = (f32[3,28,1024]{2,1,0:T(8,128)S(1)}, f32[3,28,1024]{2,1,0:T(8,128)S(1)}, u32[]{:S(2)}, u32[]{:S(2)}) collective-permute-start(f32[3,28,1024]{2,1,0:T(8,128)S(1)} %get-tuple-element.104), channel_id=1, source_target_pairs={{16,0},{32,16},{48,32},{64,48},{80,64},{96,80},{112,96},{0,112},{1... | collective-permute-start | bytes 1032200 | tf_op jit(solution)/shard_map/ppermute | solution.py:784
  6.8 25.3 %collective-permute-start = (f32[3,28,1024]{2,1,0:T(8,128)S(1)}, f32[3,28,1024]{2,1,0:T(8,128)S(1)}, u32[]{:S(2)}, u32[]{:S(2)}) collective-permute-start(f32[3,28,1024]{2,1,0:T(8,128)S(1)} %get-tuple-element.105), channel_id=1, source_target_pairs={{0,16},{16,32},{32,48},{48,64},{64,80},{80,96},{96,112},{112,0},{1... | collective-permute-start | bytes 1032200 | tf_op jit(solution)/shard_map/ppermute | solution.py:779
  10.7 20.7 %all-to-all-start = ((f32[128,1,256]{2,1,0:T(1,128)}), f32[128,1,256]{2,1,0:T(1,128)S(1)}, u32[]{:S(2)}, u32[]{:S(2)}) async-start(f32[128,1,256]{2,1,0:T(1,128)} %copy.14), calls=%async_computation | async-start | bytes 262144 | tf_op jit(solution)/shard_map/all_to_all | solution.py:798
  32.1 24.9 %copy-start.6 = (f32[3,28,1024]{2,1,0:T(8,128)}, f32[3,28,1024]{2,1,0:T(8,128)S(1)}, u32[]{:S(2)}) copy-start(f32[3,28,1024]{2,1,0:T(8,128)S(1)} %collective-permute-done.1.x_high_first) | copy-start | bytes 1032196
  32.1 0.8 copy-start.7
  32.9 19.0 %collective-permute-start.4 = (f32[136,1024]{1,0:T(8,128)}, f32[136,1024]{1,0:T(8,128)S(1)}, u32[]{:S(2)}, u32[]{:S(2)}) collective-permute-start(f32[136,1024]{1,0:T(8,128)} %get-tuple-element.64), channel_id=1, source_target_pairs={{0,1},{1,2},{2,3},{3,4},{4,5},{5,6},{6,7},{7,8},{8,9},{9,10},{10,1... | collective-permute-start | bytes 1671176 | tf_op jit(solution)/shard_map/ppermute | solution.py:779
  33.5 18.4 %collective-permute-start.5 = (f32[136,1024]{1,0:T(8,128)}, f32[136,1024]{1,0:T(8,128)S(1)}, u32[]{:S(2)}, u32[]{:S(2)}) collective-permute-start(f32[136,1024]{1,0:T(8,128)} %get-tuple-element.65), channel_id=1, source_target_pairs={{1,0},{2,1},{3,2},{4,3},{5,4},{6,5},{7,6},{8,7},{9,8},{10,9},{11,1... | collective-permute-start | bytes 1671176 | tf_op jit(solution)/shard_map/ppermute | solution.py:784
  33.5 15.1 %collective-permute-start.2 = (f32[56,1024]{1,0:T(8,128)}, f32[56,1024]{1,0:T(8,128)S(1)}, u32[]{:S(2)}, u32[]{:S(2)}) collective-permute-start(f32[56,1024]{1,0:T(8,128)} %get-tuple-element.62), channel_id=1, source_target_pairs={{0,16},{16,32},{32,48},{48,64},{64,80},{80,96},{96,112},{112,0},{1... | collective-permute-start | bytes 688136 | tf_op jit(solution)/shard_map/ppermute | solution.py:779
  34.0 17.8 %collective-permute-start.3 = (f32[56,1024]{1,0:T(8,128)}, f32[56,1024]{1,0:T(8,128)S(1)}, u32[]{:S(2)}, u32[]{:S(2)}) collective-permute-start(f32[56,1024]{1,0:T(8,128)} %get-tuple-element.63), channel_id=1, source_target_pairs={{16,0},{32,16},{48,32},{64,48},{80,64},{96,80},{112,96},{0,112},{1... | collective-permute-start | bytes 688136 | tf_op jit(solution)/shard_map/ppermute | solution.py:784
  48.6 11.1 %copy-start.8 = (f32[56,1024]{1,0:T(8,128)}, f32[56,1024]{1,0:T(8,128)S(1)}, u32[]{:S(2)}) copy-start(f32[56,1024]{1,0:T(8,128)S(1)} %collective-permute-done.2.x_low) | copy-start | bytes 688132
  51.9 0.7 copy-start.9
  51.9 2.2 %copy-start.1 = (f32[136,1024]{1,0:T(8,128)}, f32[136,1024]{1,0:T(8,128)S(1)}, u32[]{:S(2)}) copy-start(f32[136,1024]{1,0:T(8,128)S(1)} %collective-permute-done.4.y_low) | copy-start | bytes 1671172
  52.5 1.5 copy-start.2
  52.5 4.4 %collective-permute-start.7 = (f32[16,2048]{1,0:T(8,128)}, f32[16,2048]{1,0:T(8,128)S(1)}, u32[]{:S(2)}, u32[]{:S(2)}) collective-permute-start(f32[16,2048]{1,0:T(8,128)} %get-tuple-element.66), channel_id=1, source_target_pairs={{16,0},{32,16},{48,32},{64,48},{80,64},{96,80},{112,96},{0,112},{1... | collective-permute-start | bytes 393224 | tf_op jit(solution)/shard_map/ppermute | solution.py:784
  53.6 6.1 %collective-permute-start.6 = (f32[16,2048]{1,0:T(8,128)}, f32[16,2048]{1,0:T(8,128)S(1)}, u32[]{:S(2)}, u32[]{:S(2)}) collective-permute-start(f32[16,2048]{1,0:T(8,128)} %get-tuple-element.66), channel_id=1, source_target_pairs={{0,16},{16,32},{32,48},{48,64},{64,80},{80,96},{96,112},{112,0},{1... | collective-permute-start | bytes 393224 | tf_op jit(solution)/shard_map/ppermute | solution.py:779
  60.7 7.1 %copy-start = (f32[3,16,2048]{2,1,0:T(8,128)}, f32[3,16,2048]{2,1,0:T(8,128)S(1)}, u32[]{:S(2)}) copy-start(f32[3,16,2048]{2,1,0:T(8,128)S(1)} %pad_maximum_fusion.mid_ref) | copy-start | bytes 1179652
  61.0 21.3 %collective-permute-start.9 = (f32[3,16,2048]{2,0,1:T(4,128)S(1)}, f32[3,16,2048]{2,0,1:T(4,128)S(1)}, u32[]{:S(2)}, u32[]{:S(2)}) collective-permute-start(f32[3,16,2048]{2,0,1:T(4,128)S(1)} %copy.15), channel_id=1, source_target_pairs={{1,0},{2,1},{3,2},{4,3},{5,4},{6,5},{7,6},{8,7},{9,8},{10,9},{11,1... | collective-permute-start | bytes 1179656 | tf_op jit(solution)/shard_map/ppermute | solution.py:784
  63.3 19.0 %collective-permute-start.8 = (f32[3,16,2048]{2,0,1:T(4,128)S(1)}, f32[3,16,2048]{2,0,1:T(4,128)S(1)}, u32[]{:S(2)}, u32[]{:S(2)}) collective-permute-start(f32[3,16,2048]{2,0,1:T(4,128)S(1)} %copy.15), channel_id=1, source_target_pairs={{0,1},{1,2},{2,3},{3,4},{4,5},{5,6},{6,7},{7,8},{8,9},{9,10},{10,1... | collective-permute-start | bytes 1179656 | tf_op jit(solution)/shard_map/ppermute | solution.py:779
  63.3 38.2 %collective-permute-start.10 = (f32[192,1024]{1,0:T(8,128)}, f32[192,1024]{1,0:T(8,128)S(1)}, u32[]{:S(2)}, u32[]{:S(2)}) collective-permute-start(f32[192,1024]{1,0:T(8,128)} %get-tuple-element.80), channel_id=1, source_target_pairs={{0,16},{16,32},{32,48},{48,64},{64,80},{80,96},{96,112},{112,0},{1... | collective-permute-start | bytes 2359304 | tf_op jit(solution)/shard_map/ppermute | solution.py:779
  63.5 39.9 %collective-permute-start.11 = (f32[192,1024]{1,0:T(8,128)}, f32[192,1024]{1,0:T(8,128)S(1)}, u32[]{:S(2)}, u32[]{:S(2)}) collective-permute-start(f32[192,1024]{1,0:T(8,128)} %get-tuple-element.81), channel_id=1, source_target_pairs={{16,0},{32,16},{48,32},{64,48},{80,64},{96,80},{112,96},{0,112},{1... | collective-permute-start | bytes 2359304 | tf_op jit(solution)/shard_map/ppermute | solution.py:784
  101.5 2.0 %copy-start.4 = (f32[192,1024]{1,0:T(8,128)}, f32[192,1024]{1,0:T(8,128)S(1)}, u32[]{:S(2)}) copy-start(f32[192,1024]{1,0:T(8,128)S(1)} %collective-permute-done.10.x_low_late) | copy-start | bytes 2359300
  103.5 0.9 copy-start.5
  140.8 8.5 %collective-permute-start.12 = (f32[9,2048]{1,0:T(8,128)}, f32[9,2048]{1,0:T(8,128)S(1)}, u32[]{:S(2)}, u32[]{:S(2)}) collective-permute-start(f32[9,2048]{1,0:T(8,128)} %get-tuple-element.98), channel_id=1, source_target_pairs={{1,0},{2,1},{3,2},{4,3},{5,4},{6,5},{7,6},{8,7},{9,8},{10,9},{11,1... | collective-permute-start | bytes 221192 | tf_op jit(solution)/shard_map/ppermute | solution.py:784
  142.2 7.1 %collective-permute-start.13 = (f32[9,2048]{1,0:T(8,128)}, f32[9,2048]{1,0:T(8,128)S(1)}, u32[]{:S(2)}, u32[]{:S(2)}) collective-permute-start(f32[9,2048]{1,0:T(8,128)} %get-tuple-element.99), channel_id=1, source_target_pairs={{0,1},{1,2},{2,3},{3,4},{4,5},{5,6},{6,7},{7,8},{8,9},{9,10},{10,1... | collective-permute-start | bytes 221192 | tf_op jit(solution)/shard_map/ppermute | solution.py:779
  149.3 12.9 %copy-start.3 = (f32[9,2048]{1,0:T(8,128)}, f32[9,2048]{1,0:T(8,128)S(1)}, u32[]{:S(2)}) copy-start(f32[9,2048]{1,0:T(8,128)S(1)} %add.11.sides_ref) | copy-start | bytes 221188
  150.3 12.0 %collective-permute-start.14 = (f32[3,2048]{1,0:T(4,128)S(1)}, f32[3,2048]{1,0:T(4,128)S(1)}, u32[]{:S(2)}, u32[]{:S(2)}) collective-permute-start(f32[3,2048]{1,0:T(4,128)S(1)} %get-tuple-element.101), channel_id=1, source_target_pairs={{16,0},{32,16},{48,32},{64,48},{80,64},{96,80},{112,96},{0,112},{1... | collective-permute-start | bytes 73736 | tf_op jit(solution)/shard_map/ppermute | solution.py:784
  155.1 7.2 %collective-permute-start.15 = (f32[3,2048]{1,0:T(4,128)S(1)}, f32[3,2048]{1,0:T(4,128)S(1)}, u32[]{:S(2)}, u32[]{:S(2)}) collective-permute-start(f32[3,2048]{1,0:T(4,128)S(1)} %get-tuple-element.102), channel_id=1, source_target_pairs={{0,16},{16,32},{32,48},{48,64},{64,80},{80,96},{96,112},{112,0},{1... | collective-permute-start | bytes 73736 | tf_op jit(solution)/shard_map/ppermute | solution.py:779
  162.3 0.6 copy-start.10
  162.3 0.6 copy-start.11
